TPU v7x, 256 devices: a whole 4x4x8 slice. The times are simulated.
256 devices in a mesh: row: 16 (over y_hi, x, core), col: 8 (over z), rep: 2 (over y_lo).
Axes of the slice: x: 4, y: 4 (y_hi: 2, y_lo: 2; y = y_hi * 2 + y_lo), z: 8, core: 2. Of those that a mesh axis runs over, the one named last changes fastest.
Arguments:
- features: bfloat16 [32768, 512], P(('row', 'col', 'rep')), may hold values from -6 to 6
- tile_values: bfloat16 [32768, 128, 128], P(('row', 'col', 'rep')), as said below
- tile_coords: int32 [32768, 2], P(('row', 'col', 'rep')), may hold values from 0 to 15, as said below
- tile_counts: int32 [256], P(('row', 'col', 'rep')), may hold values from 16 to 128, as said below
- weight: bfloat16 [512, 512], replicated, may hold values from -0.25 to 0.25
- cotangent: bfloat16 [32768, 512], P(('row', 'col', 'rep')), may hold values from -6 to 6
Outputs:
- activations: bfloat16 [32768, 512], P(('row', 'col', 'rep'))
- grad_features: bfloat16 [32768, 512], P(('row', 'col', 'rep'))
- grad_weight: float32 [512, 512], replicated
Inputs may be any that keep to these rules, and one draw needn't show every extreme that they name: `tile_values`: nonnegative edge weights; slots past a block's live count hold values that must be ignored. `tile_coords`: column 0 is a tile row below 16, column 1 a tile column below 16; within one block no tile position appears twice. `tile_counts`: live slots differ from block to block; some block uses all 128 slots.
All inputs are finite; a program needn't handle non-finite values.
Results may differ from a plain program's by a relative error of at most 0.028.
Values may be sent and summed in bfloat16 or wider, within the bound.
No kernel may reach another device: no remote copies, remote signals or barrier semaphores. Data moves between devices by JAX's collectives and lax.ppermute only.
A program may use at most 128 MiB of HBM per device.

v0:
```python
import jax
import jax.numpy as jnp
from jax import lax
from jax.experimental import pallas as pl
from jax.experimental.pallas import tpu as pltpu
from jax.sharding import PartitionSpec as P

TILE = 128
BUNCH = 16
SIDE = 2048
BLOCK = 256
F32 = jnp.float32
BF16 = jnp.bfloat16
MIB = 1024 * 1024
SCOPED = 8 * MIB
WHOLE = pl.BlockSpec(memory_space=pltpu.VMEM)


def wide_sum(*terms):
    total = terms[0].astype(F32)
    for term in terms[1:]:
        total = total + term.astype(F32)
    return total.astype(BF16)


def fence(*values):
    return lax.optimization_barrier(values)


def stack(*values):
    return jnp.concatenate(values, 0)


def dense_kernel(counts_ref, places_ref, tiles_ref, dense_ref, held_ref, arrived):
    bunches = held_ref.shape[0] // BUNCH

    def fetch(b):
        part = pl.ds(b * BUNCH, BUNCH)
        return pltpu.make_async_copy(tiles_ref.at[part], held_ref.at[part], arrived.at[b])

    for b in range(bunches):
        fetch(b).start()

    def clear(r, carry):
        dense_ref[pl.ds(pl.multiple_of(r * TILE, TILE), TILE), :] = jnp.zeros((TILE, SIDE), BF16)
        return carry

    lax.fori_loop(0, SIDE // TILE, clear, 0)
    live = counts_ref[0]
    for b in range(bunches):
        fetch(b).wait()

        def place(j, carry, b=b):
            slot = b * BUNCH + j

            @pl.when(slot < live)
            def _():
                top = pl.multiple_of(places_ref[2 * slot] * TILE, TILE)
                left = pl.multiple_of(places_ref[2 * slot + 1] * TILE, TILE)
                dense_ref[pl.ds(top, TILE), pl.ds(left, TILE)] = held_ref[slot]

            return carry

        lax.fori_loop(0, BUNCH, place, 0)


def dense_block(tile_values, places, tile_counts):
    slots = tile_values.shape[0]
    smem = pl.BlockSpec(memory_space=pltpu.SMEM)
    return pl.pallas_call(
        dense_kernel,
        out_shape=jax.ShapeDtypeStruct((SIDE, SIDE), BF16),
        in_specs=[smem, smem, pl.BlockSpec(memory_space=pltpu.HBM)],
        out_specs=WHOLE,
        scratch_shapes=[
            pltpu.VMEM(tile_values.shape, BF16),
            pltpu.SemaphoreType.DMA((slots // BUNCH,)),
        ],
        compiler_params=pltpu.CompilerParams(vmem_limit_bytes=SCOPED),
        cost_estimate=pl.CostEstimate(flops=0, bytes_accessed=12 * MIB, transcendentals=0),
        name="dense_build",
    )(tile_counts, places, tile_values)


def rows_kernel(first, dense_ref, *refs):
    pieces, (out_ref, panel_ref) = refs[:-2], refs[-2:]
    at = 0
    for piece in pieces:
        panel_ref[at : at + piece.shape[0], :] = piece[...]
        at += piece.shape[0]

    def product(i, carry):
        start = pl.multiple_of((first + i * BLOCK) & (SIDE - 1), BLOCK)
        out_ref[pl.ds(pl.multiple_of(i * BLOCK, BLOCK), BLOCK), :] = jnp.dot(
            dense_ref[pl.ds(start, BLOCK), :], panel_ref[...], preferred_element_type=F32
        ).astype(BF16)
        return carry

    lax.fori_loop(0, out_ref.shape[0] // BLOCK, product, 0)


def rows_dot(dense, pieces, first, rows, name):
    width = pieces[0].shape[1]
    return pl.pallas_call(
        lambda *refs: rows_kernel(first, *refs),
        out_shape=jax.ShapeDtypeStruct((rows, width), BF16),
        in_specs=[WHOLE] * (1 + len(pieces)),
        out_specs=WHOLE,
        scratch_shapes=[pltpu.VMEM((SIDE, width), BF16)],
        compiler_params=pltpu.CompilerParams(vmem_limit_bytes=SCOPED),
        cost_estimate=pl.CostEstimate(
            flops=2 * rows * SIDE * width, bytes_accessed=2 * rows * SIDE, transcendentals=0
        ),
        name=name,
    )(dense, *pieces)


def columns_kernel(first, dense_ref, *refs):
    pieces, (out_ref, panel_ref) = refs[:-2], refs[-2:]
    width = panel_ref.shape[0]
    down, across = 0, 0
    for piece in pieces:
        depth, step = piece.shape
        panel_ref[down : down + depth, across : across + step] = piece[...]
        down += depth
        if down == width:
            down, across = 0, across + step

    def product(i, carry):
        for j in range(2):
            begin = pl.multiple_of(first + (2 * i + j) * BLOCK, BLOCK)
            result = jnp.dot(
                panel_ref[...], dense_ref[:, pl.ds(begin, BLOCK)], preferred_element_type=F32
            ).astype(BF16)
            out_ref[4 * i + 2 * j] = result[:, :TILE]
            out_ref[4 * i + 2 * j + 1] = result[:, TILE:]
        return carry

    lax.fori_loop(0, out_ref.shape[0] // 4, product, 0)


def columns_dot(dense, pieces, first, blocks, name):
    width = pieces[0].shape[0]
    return pl.pallas_call(
        lambda *refs: columns_kernel(first, *refs),
        out_shape=jax.ShapeDtypeStruct((blocks, width, TILE), BF16),
        in_specs=[WHOLE] * (1 + len(pieces)),
        out_specs=WHOLE,
        scratch_shapes=[pltpu.VMEM((width, SIDE), BF16)],
        compiler_params=pltpu.CompilerParams(vmem_limit_bytes=SCOPED),
        cost_estimate=pl.CostEstimate(
            flops=2 * blocks * TILE * SIDE * width,
            bytes_accessed=2 * blocks * TILE * SIDE,
            transcendentals=0,
        ),
        name=name,
    )(dense, *pieces)


def layer_kernel(mine_ref, theirs_ref, weight_ref, cot_ref, twin_ref, agg_ref, act_ref, pre_grad_ref, grad_ref):
    half = cot_ref.shape[0]
    for at, cot in ((0, cot_ref), (half, twin_ref)):
        rows = slice(at, at + half)
        total = mine_ref[rows, :].astype(F32) + theirs_ref[half - at : 2 * half - at, :].astype(F32)
        aggregated = total.astype(BF16)
        agg_ref[rows, :] = aggregated
        pre_act = jnp.dot(aggregated, weight_ref[...], preferred_element_type=F32)
        gate = 1.0 / (1.0 + jnp.exp(-pre_act))
        if at == 0:
            act_ref[...] = (pre_act * gate).astype(BF16)
        slope = gate * (1.0 + pre_act * (1.0 - gate))
        pre_grad = (cot[...].astype(F32) * slope).astype(BF16)
        pre_grad_ref[rows, :] = pre_grad
        grad_ref[:, rows] = lax.dot_general(
            weight_ref[...], pre_grad, (((1,), (1,)), ((), ())), preferred_element_type=F32
        ).astype(BF16)


def layer(mine, theirs, weight, cotangent, cot_twin):
    rows, width = cotangent.shape
    both = jax.ShapeDtypeStruct((2 * rows, width), BF16)
    own = jax.ShapeDtypeStruct((rows, width), BF16)
    turned = jax.ShapeDtypeStruct((width, 2 * rows), BF16)
    return pl.pallas_call(
        layer_kernel,
        out_shape=(both, own, both, turned),
        in_specs=[WHOLE] * 5,
        out_specs=(WHOLE,) * 4,
        compiler_params=pltpu.CompilerParams(vmem_limit_bytes=SCOPED),
        name="layer",
    )(mine, theirs, weight, cotangent, cot_twin)


def finish_kernel(*refs):
    total = refs[0][...].astype(F32)
    for part in refs[1:-1]:
        total = total + part[...].astype(F32)
    refs[-1][...] = total.T.astype(BF16)


def finish(*parts):
    width, rows = parts[0].shape
    return pl.pallas_call(
        finish_kernel,
        out_shape=jax.ShapeDtypeStruct((rows, width), BF16),
        in_specs=[WHOLE] * len(parts),
        out_specs=WHOLE,
        compiler_params=pltpu.CompilerParams(vmem_limit_bytes=SCOPED),
        name="finish",
    )(*parts)


def weight_part_kernel(where_ref, agg_ref, pre_grad_ref, kept_ref, sent_ref):
    low, core = where_ref[0], where_ref[1]

    def rows_of(which):
        at = pl.multiple_of(low * 256 + which * 128, 128)
        return lax.dot_general(
            agg_ref[:, pl.ds(at, 128)],
            pre_grad_ref[...],
            (((0,), (0,)), ((), ())),
            preferred_element_type=F32,
        )

    kept_ref[...] = rows_of(core)
    sent_ref[...] = rows_of(1 - core).astype(BF16)


def weight_part(where, aggregated, pre_grad):
    width = pre_grad.shape[1]
    return pl.pallas_call(
        weight_part_kernel,
        out_shape=(
            jax.ShapeDtypeStruct((128, width), F32),
            jax.ShapeDtypeStruct((128, width), BF16),
        ),
        in_specs=[pl.BlockSpec(memory_space=pltpu.SMEM)] + [WHOLE] * 2,
        out_specs=(WHOLE,) * 2,
        compiler_params=pltpu.CompilerParams(vmem_limit_bytes=SCOPED),
        name="weight_part",
    )(where, aggregated, pre_grad)


def weight_place_kernel(norm, where_ref, own_ref, core_ref, rep_ref, both_ref, out_ref):
    low, core = where_ref[0], where_ref[1]
    rows = own_ref.shape[0]
    for value, at_low, at_core in (
        (own_ref, low, core),
        (core_ref, low, 1 - core),
        (rep_ref, 1 - low, core),
        (both_ref, 1 - low, 1 - core),
    ):
        at = pl.multiple_of((at_low * 2 + at_core) * rows, rows)
        out_ref[pl.ds(at, rows), :] = value[...].astype(F32) * norm


def weight_place(where, blocks, norm):
    rows, width = blocks[0].shape
    return pl.pallas_call(
        lambda *refs: weight_place_kernel(norm, *refs),
        out_shape=jax.ShapeDtypeStruct((4 * rows, width), F32),
        in_specs=[pl.BlockSpec(memory_space=pltpu.SMEM)] + [WHOLE] * 4,
        out_specs=WHOLE,
        compiler_params=pltpu.CompilerParams(vmem_limit_bytes=SCOPED),
        name="weight_place",
    )(where, *blocks)


def swap_row(value, mask):
    return lax.ppermute(value, "row", [(r, r ^ mask) for r in range(16)])


def swap_core(value):
    return swap_row(value, 1)


def along_x(value, step):
    def target(r):
        return (r & 9) | ((((r >> 1) + step) & 3) << 1)

    return lax.ppermute(value, "row", [(r, target(r)) for r in range(16)])


def along_z(value, step):
    return lax.ppermute(value, "col", [(z, (z + step) % 8) for z in range(8)])


def swap_z(value, mask):
    return lax.ppermute(value, "col", [(z, z ^ mask) for z in range(8)])


def swap_rep(value):
    return lax.ppermute(value, "rep", [(0, 1), (1, 0)])


def swap_core_rep(value):
    pairs = [(2 * r + low, 2 * (r ^ 1) + 1 - low) for r in range(16) for low in range(2)]
    return lax.ppermute(value, ("row", "rep"), pairs)


LATE = ((1, 1), (3, 1), (2, 0), (2, 1))
SOON = ((0, 1), (1, 0), (3, 0))
ORDER = [(x, y, 1) for x, y in LATE] + [(x, y, 0) for x, y in LATE]
ORDER += [(x, y, 1) for x, y in SOON] + [(x, y, 0) for x, y in SOON]
ORDER += [(0, 0, 1), (0, 0, 0)]


def column_places(tile_columns):
    me = lax.axis_index("row")
    half, x, core = me >> 3, (me >> 1) & 3, me & 1
    dy = (tile_columns >> 3) ^ half
    dx = (((tile_columns >> 1) & 3) - x) & 3
    dc = (tile_columns & 1) ^ core
    key = dx * 4 + dy * 2 + dc
    place = jnp.zeros_like(key)
    for at, (bx, by, bc) in enumerate(ORDER):
        place = jnp.where(key == bx * 4 + by * 2 + bc, at, place)
    return place


def row_places(tile_rows):
    z, low = lax.axis_index("col"), lax.axis_index("rep")
    dz = ((tile_rows >> 1) - z) & 7
    return 2 * dz + ((tile_rows & 1) ^ low)


def body(features, tile_values, tile_coords, tile_counts, weight, cotangent):
    nodes = features.shape[0] * 256
    where = jnp.stack([lax.axis_index("rep"), lax.axis_index("row") & 1]).astype(jnp.int32)
    places = jnp.stack([row_places(tile_coords[:, 0]), column_places(tile_coords[:, 1])], -1)
    places = places.reshape(-1)

    half = swap_row(features, 8)
    left = along_x(features, 1)
    right = along_x(features, -1)
    core = swap_core(features)
    half, left, right, core, places, where = fence(half, left, right, core, places, where)
    sides = swap_row(stack(right, left), 8)
    far_half = swap_row(half, 4)
    far = along_x(left, 1)
    core_soon = swap_core(stack(half, right, left))
    dense = dense_block(tile_values, places, tile_counts)
    sides, far, far_half, core_soon, dense = fence(sides, far, far_half, core_soon, dense)
    late = stack(sides, far, far_half)
    core_late = swap_core(late)
    cot_twin = swap_rep(cotangent)
    pieces = (core_late, late, core_soon, half, right, left, core, features)

    middle = rows_dot(dense, pieces, 1024, 256, "rows_middle")
    up, down, middle = fence(middle[:128], middle[128:], middle)
    up, down = along_z(up, 1), along_z(down, -1)
    rest = rows_dot(dense, pieces, 1280, 1792, "rows_rest")

    def block(d):
        at = (d - 5) % 8 * 256
        return rest[at : at + 256]

    ahead, behind = block(3), block(5)
    up = stack(wide_sum(ahead[:128], up), ahead[128:])
    down = stack(behind[:128], wide_sum(behind[128:], down))
    up, down, cot_twin = fence(up, down, cot_twin)
    up, down = along_z(up, 1), along_z(down, -1)
    up, down = fence(up, down)
    up, down = fence(wide_sum(block(2), up), wide_sum(block(6), down))
    up, down = along_z(up, 1), along_z(down, -1)
    up, down = fence(up, down)
    up, down = fence(wide_sum(block(1), up), wide_sum(block(7), down))
    up, down = along_z(up, 1), along_z(down, -1)
    mine = wide_sum(block(0), up, down)
    theirs = swap_rep(mine)
    aggregated, activations, pre_grad, here = layer(mine, theirs, weight, cotangent, cot_twin)

    here, aggregated, pre_grad = fence(here, aggregated, pre_grad)
    below, above = along_z(here, 1), along_z(here, -1)
    kept, sent = weight_part(where, aggregated, pre_grad)
    taken = swap_core(sent)
    near = below, above

    below, above, taken = fence(below, above, taken)
    share = wide_sum(kept, taken)
    below, above, share = fence(below, above, share)
    below, above = along_z(below, 1), along_z(above, -1)
    taken = [swap_row(share, 2 * m) for m in (1, 2, 3)]
    next_near = below, above

    below, above, *taken = fence(below, above, *taken)
    share = (share.astype(F32) + taken[0].astype(F32)) + (taken[1].astype(F32) + taken[2].astype(F32))
    share = share.astype(BF16)
    below, above, share = fence(below, above, share)
    below, above = along_z(below, 1), along_z(above, -1)
    taken = swap_row(share, 8)
    far = below, above

    below, above, taken = fence(below, above, taken)
    share = wide_sum(share, taken)
    below, above, share = fence(below[:256], above[256:], share)
    below, above = along_z(below, 1), along_z(above, -1)
    taken = swap_z(share, 1)
    below, above, taken = fence(below, above, taken)
    share = wide_sum(share, taken)
    rows = (here, near[1], next_near[1], far[1], below, above, far[0], next_near[0], near[0])

    other = columns_dot(dense, rows, 0, 4, "columns_other")
    other, share = fence(other, share)
    other = swap_core(other)
    taken = swap_z(share, 2)
    rest = columns_dot(dense, rows, 512, 12, "columns_rest")
    other, rest, taken = fence(other, rest, taken)
    late = wide_sum(rest[:4], other)
    share = wide_sum(share, taken)
    late, soon, share = fence(late, rest[4:7], share)
    sides = swap_row(late[:2], 8)
    far_half = swap_row(late[3], 4)
    far = along_x(late[2], -1)
    soon = swap_core(soon)
    taken = swap_z(share, 4)

    sides, far_half, far, soon, taken = fence(sides, far_half, far, soon, taken)
    half = wide_sum(rest[7], soon[0], far_half)
    right = wide_sum(rest[8], soon[1], sides[0])
    left = wide_sum(rest[9], soon[2], sides[1], far)
    share = wide_sum(share, taken)
    half, right, left, core, share = fence(half, right, left, rest[10], share)
    half, right, left = swap_row(half, 8), along_x(right, 1), along_x(left, -1)
    core = swap_core(core)
    shares = share, swap_core(share), swap_rep(share), swap_core_rep(share)
    grad_weight = weight_place(where, shares, 1.0 / nodes**0.5)
    grad_features = finish(rest[11], half, right, left, core)
    return (activations, grad_features, grad_weight)


def solution(mesh):
    split = ("row", "col", "rep")
    placed = (P(split, None), P(split, None, None), P(split, None), P(split), P(), P(split, None))
    return jax.shard_map(
        body,
        mesh=mesh,
        in_specs=placed,
        out_specs=(P(split, None), P(split, None), P()),
        check_vma=False,
    )
```

profile of v0, /device:TPU:1, one launch (start us, length us, event | category | flops | bytes accessed | tf_op | source)
XLA Modules:
  0.0 152.4 jit_solution(11668217802594313607)
XLA Ops:
  0.6 3.3 %collective-permute-start.3 = (bf16[128,512]{1,0:T(8,128)(2,1)}, bf16[128,512]{1,0:T(8,128)(2,1)S(1)}, u32[]{:S(2)}, u32[]{:S(2)}) collective-permute-start(bf16[128,512]{1,0:T(8,128)(2,1)} %refs_8_.3), channel_id=1, source_target_pairs={{0,16},{16,0},{32,48},{48,32},{64,80},{80,64},{96,112},{112,96},{1... | collective-permute-start | bytes 393224 | tf_op jit(solution)/shard_map/ppermute | solution.py:270
  4.0 0.8 collective-permute-start.2
  4.7 0.7 collective-permute-start.1
  5.4 2.2 %collective-permute-start = (bf16[128,512]{1,0:T(8,128)(2,1)}, bf16[128,512]{1,0:T(8,128)(2,1)S(1)}, u32[]{:S(2)}, u32[]{:S(2)}) collective-permute-start(bf16[128,512]{1,0:T(8,128)(2,1)} %refs_8_.3), channel_id=1, source_target_pairs={{0,128},{16,144},{32,160},{48,176},{64,192},{80,208},{96,224},{112... | collective-permute-start | bytes 393224 | tf_op jit(solution)/shard_map/ppermute | solution.py:270
  7.6 0.8 xor_add_fusion
  9.2 1.6 %collective-permute-done.1.refs_6_ = bf16[128,512]{1,0:T(8,128)(2,1)S(1)} collective-permute-done((bf16[128,512]{1,0:T(8,128)(2,1)}, bf16[128,512]{1,0:T(8,128)(2,1)S(1)}, u32[]{:S(2)}, u32[]{:S(2)}) %collective-permute-start.1) | collective-permute-done | bytes 131104 | tf_op jit(solution)/shard_map/ppermute | solution.py:281
  10.9 0.7 collective-permute-done.refs_4_
  11.6 1.6 %collective-permute-start.7 = (bf16[384,512]{1,0:T(8,128)(2,1)S(1)}, bf16[384,512]{1,0:T(8,128)(2,1)S(1)}, u32[]{:S(2)}, u32[]{:S(2)}) collective-permute-start(bf16[384,512]{1,0:T(8,128)(2,1)S(1)} %pad_maximum_fusion), channel_id=1, source_target_pairs={{0,16},{16,0},{32,48},{48,32},{64,80},{80,64},{96,112},{112,96},{1... | collective-permute-start | bytes 1179656 | tf_op jit(solution)/shard_map/ppermute | solution.py:270
  13.2 2.3 %collective-permute-start.4 = (bf16[256,512]{1,0:T(8,128)(2,1)S(1)}, bf16[256,512]{1,0:T(8,128)(2,1)S(1)}, u32[]{:S(2)}, u32[]{:S(2)}) collective-permute-start(bf16[256,512]{1,0:T(8,128)(2,1)S(1)} %pad_maximum_fusion.1), channel_id=1, source_target_pairs={{0,128},{16,144},{32,160},{48,176},{64,192},{80,208},{96,224},{112... | collective-permute-start | bytes 786440 | tf_op jit(solution)/shard_map/ppermute | solution.py:270
  15.5 1.7 %collective-permute-start.6 = (bf16[128,512]{1,0:T(8,128)(2,1)S(1)}, bf16[128,512]{1,0:T(8,128)(2,1)S(1)}, u32[]{:S(2)}, u32[]{:S(2)}) collective-permute-start(bf16[128,512]{1,0:T(8,128)(2,1)S(1)} %collective-permute-done.refs_4_), channel_id=1, source_target_pairs={{0,64},{16,80},{32,96},{48,112},{64,0},{80,16},{96,32},{112,48},{1... | collective-permute-start | bytes 393224 | tf_op jit(solution)/shard_map/ppermute | solution.py:270
  17.2 1.5 collective-permute-start.5
  19.4 2.2 %copy-done = bf16[128,128,128]{2,1,0:T(8,128)(2,1)S(1)} copy-done((bf16[128,128,128]{2,1,0:T(8,128)(2,1)S(1)}, bf16[128,128,128]{2,1,0:T(8,128)(2,1)}, u32[]{:S(2)}) %copy-start) | copy-done | bytes 4194328
  21.6 3.6 %dense_build.1.refs_0_ = bf16[2048,2048]{1,0:T(8,128)(2,1)S(1)} custom-call(s32[1]{0:T(128)S(6)} %copy.12.counts_ref, s32[256]{0:T(256)S(1)} %reshape.23.places_ref, bf16[128,128,128]{2,1,0:T(8,128)(2,1)S(1)} %copy-done), custom_call_target="tpu_custom_call" | custom-call | bytes 12582912 | tf_op jit(solution)/shard_map/dense_build/pallas_call | solution.py:70
  25.3 0.9 collective-permute-start.8
  26.6 1.0 collective-permute-done.8.refs_1_
  27.7 0.7 rows_middle.1
  28.4 1.7 %collective-permute-start.9 = (bf16[128,512]{1,0:T(8,128)(2,1)S(1)}, bf16[128,512]{1,0:T(8,128)(2,1)S(1)}, u32[]{:S(2)}, u32[]{:S(2)}) collective-permute-start(bf16[128,512]{1,0:T(8,128)(2,1)S(1)} %get-tuple-element.87), channel_id=1, source_target_pairs={{0,2},{2,4},{4,6},{6,8},{8,10},{10,12},{12,14},{14,0},{1,3},{3,5},... | collective-permute-start | bytes 393224 | tf_op jit(solution)/shard_map/ppermute | solution.py:285
  30.1 3.9 %collective-permute-start.10 = (bf16[128,512]{1,0:T(8,128)(2,1)S(1)}, bf16[128,512]{1,0:T(8,128)(2,1)S(1)}, u32[]{:S(2)}, u32[]{:S(2)}) collective-permute-start(bf16[128,512]{1,0:T(8,128)(2,1)S(1)} %get-tuple-element.88), channel_id=1, source_target_pairs={{0,14},{2,0},{4,2},{6,4},{8,6},{10,8},{12,10},{14,12},{1,15},{3,1}... | collective-permute-start | bytes 393224 | tf_op jit(solution)/shard_map/ppermute | solution.py:285
  34.0 5.1 %rows_rest.1 = bf16[1792,512]{1,0:T(8,128)(2,1)S(1)} custom-call(bf16[2048,2048]{1,0:T(8,128)(2,1)S(1)} %dense_build.1.refs_0_, bf16[512,512]{1,0:T(8,128)(2,1)S(1)} %collective-permute-done.8.refs_1_, bf16[512,512]{1,0:T(8,128)(2,1)S(1)} %constant_dynamic-update-slice_fusion.refs_2_, bf16[384,512]{1,0:T(8,128)(2,1)S(1)} %collective-permute-done.7.refs_3_, ...), custom_call_target="tpu_custom_call" | custom-call | flops 3758096384 | bytes 7340032 | tf_op jit(solution)/shard_map/rows_rest/pallas_call | solution.py:104
  39.4 2.7 %collective-permute-start.13 = (bf16[256,512]{1,0:T(8,128)(2,1)S(1)}, bf16[256,512]{1,0:T(8,128)(2,1)S(1)}, u32[]{:S(2)}, u32[]{:S(2)}) collective-permute-start(bf16[256,512]{1,0:T(8,128)(2,1)S(1)} %get-tuple-element.90), channel_id=1, source_target_pairs={{0,14},{2,0},{4,2},{6,4},{8,6},{10,8},{12,10},{14,12},{1,15},{3,1}... | collective-permute-start | bytes 786440 | tf_op jit(solution)/shard_map/ppermute | solution.py:285
  42.0 5.7 %collective-permute-done.12 = bf16[256,512]{1,0:T(8,128)(2,1)S(1)} collective-permute-done((bf16[256,512]{1,0:T(8,128)(2,1)S(1)}, bf16[256,512]{1,0:T(8,128)(2,1)S(1)}, u32[]{:S(2)}, u32[]{:S(2)}) %collective-permute-start.12) | collective-permute-done | bytes 262176 | tf_op jit(solution)/shard_map/ppermute | solution.py:285
  48.0 2.7 %collective-permute-start.15 = (bf16[256,512]{1,0:T(8,128)(2,1)S(1)}, bf16[256,512]{1,0:T(8,128)(2,1)S(1)}, u32[]{:S(2)}, u32[]{:S(2)}) collective-permute-start(bf16[256,512]{1,0:T(8,128)(2,1)S(1)} %get-tuple-element.94), channel_id=1, source_target_pairs={{0,14},{2,0},{4,2},{6,4},{8,6},{10,8},{12,10},{14,12},{1,15},{3,1}... | collective-permute-start | bytes 786440 | tf_op jit(solution)/shard_map/ppermute | solution.py:285
  50.7 4.8 %collective-permute-done.14 = bf16[256,512]{1,0:T(8,128)(2,1)S(1)} collective-permute-done((bf16[256,512]{1,0:T(8,128)(2,1)S(1)}, bf16[256,512]{1,0:T(8,128)(2,1)S(1)}, u32[]{:S(2)}, u32[]{:S(2)}) %collective-permute-start.14) | collective-permute-done | bytes 262176 | tf_op jit(solution)/shard_map/ppermute | solution.py:285
  55.6 1.4 collective-permute-start.16
  57.0 1.3 collective-permute-start.17
  58.4 3.8 %collective-permute-done.16 = bf16[256,512]{1,0:T(8,128)(2,1)S(1)} collective-permute-done((bf16[256,512]{1,0:T(8,128)(2,1)S(1)}, bf16[256,512]{1,0:T(8,128)(2,1)S(1)}, u32[]{:S(2)}, u32[]{:S(2)}) %collective-permute-start.16) | collective-permute-done | bytes 262176 | tf_op jit(solution)/shard_map/ppermute | solution.py:285
  62.7 5.2 %collective-permute-done.18.theirs_ref = bf16[256,512]{1,0:T(8,128)(2,1)S(1)} collective-permute-done((bf16[256,512]{1,0:T(8,128)(2,1)S(1)}, bf16[256,512]{1,0:T(8,128)(2,1)S(1)}, u32[]{:S(2)}, u32[]{:S(2)}) %collective-permute-start.18) | collective-permute-done | bytes 262176 | tf_op jit(solution)/shard_map/ppermute | solution.py:293
  68.0 1.0 layer.1
  68.9 1.5 %collective-permute-start.20 = (bf16[512,256]{1,0:T(8,128)(2,1)S(1)}, bf16[512,256]{1,0:T(8,128)(2,1)S(1)}, u32[]{:S(2)}, u32[]{:S(2)}) collective-permute-start(bf16[512,256]{1,0:T(8,128)(2,1)S(1)} %get-tuple-element.104.refs_1_), channel_id=1, source_target_pairs={{0,2},{2,4},{4,6},{6,8},{8,10},{10,12},{12,14},{14,0},{1,3},{3,5},... | collective-permute-start | bytes 786440 | tf_op jit(solution)/shard_map/ppermute | solution.py:285
  70.5 1.1 collective-permute-start.19
  71.6 0.8 weight_part.1
  72.4 6.0 %collective-permute-start.21 = (bf16[128,512]{1,0:T(8,128)(2,1)S(1)}, bf16[128,512]{1,0:T(8,128)(2,1)S(1)}, u32[]{:S(2)}, u32[]{:S(2)}) collective-permute-start(bf16[128,512]{1,0:T(8,128)(2,1)S(1)} %get-tuple-element.108), channel_id=1, source_target_pairs={{0,16},{16,0},{32,48},{48,32},{64,80},{80,64},{96,112},{112,96},{1... | collective-permute-start | bytes 393224 | tf_op jit(solution)/shard_map/ppermute | solution.py:270
  78.4 1.0 collective-permute-done.21
  79.4 0.8 collective-permute-start.22
  80.2 0.7 collective-permute-start.23
  81.0 0.8 collective-permute-start.26
  81.7 0.7 collective-permute-start.25
  82.5 1.8 %collective-permute-start.24 = (bf16[128,512]{1,0:T(8,128)(2,1)S(1)}, bf16[128,512]{1,0:T(8,128)(2,1)S(1)}, u32[]{:S(2)}, u32[]{:S(2)}) collective-permute-start(bf16[128,512]{1,0:T(8,128)(2,1)S(1)} %add_convert_fusion.12), channel_id=1, source_target_pairs={{0,32},{16,48},{32,0},{48,16},{64,96},{80,112},{96,64},{112,80},{1... | collective-permute-start | bytes 393224 | tf_op jit(solution)/shard_map/ppermute | solution.py:270
  84.2 3.2 %collective-permute-done.26 = bf16[128,512]{1,0:T(8,128)(2,1)S(1)} collective-permute-done((bf16[128,512]{1,0:T(8,128)(2,1)S(1)}, bf16[128,512]{1,0:T(8,128)(2,1)S(1)}, u32[]{:S(2)}, u32[]{:S(2)}) %collective-permute-start.26) | collective-permute-done | bytes 131104 | tf_op jit(solution)/shard_map/ppermute | solution.py:270
  87.4 0.9 collective-permute-done.24
  88.4 2.0 %collective-permute-start.27 = (bf16[512,256]{1,0:T(8,128)(2,1)S(1)}, bf16[512,256]{1,0:T(8,128)(2,1)S(1)}, u32[]{:S(2)}, u32[]{:S(2)}) collective-permute-start(bf16[512,256]{1,0:T(8,128)(2,1)S(1)} %collective-permute-done.22.refs_3_), channel_id=1, source_target_pairs={{0,14},{2,0},{4,2},{6,4},{8,6},{10,8},{12,10},{14,12},{1,15},{3,1}... | collective-permute-start | bytes 786440 | tf_op jit(solution)/shard_map/ppermute | solution.py:285
  91.1 4.6 %collective-permute-done.29 = bf16[128,512]{1,0:T(8,128)(2,1)S(1)} collective-permute-done((bf16[128,512]{1,0:T(8,128)(2,1)S(1)}, bf16[128,512]{1,0:T(8,128)(2,1)S(1)}, u32[]{:S(2)}, u32[]{:S(2)}) %collective-permute-start.29) | collective-permute-done | bytes 131104 | tf_op jit(solution)/shard_map/ppermute | solution.py:270
  95.7 1.1 collective-permute-done.28.refs_7_
  97.0 2.7 %collective-permute-start.31 = (bf16[256,256]{1,0:T(8,128)(2,1)S(1)}, bf16[256,256]{1,0:T(8,128)(2,1)S(1)}, u32[]{:S(2)}, u32[]{:S(2)}) collective-permute-start(bf16[256,256]{1,0:T(8,128)(2,1)S(1)} %slice.110), channel_id=1, source_target_pairs={{0,14},{2,0},{4,2},{6,4},{8,6},{10,8},{12,10},{14,12},{1,15},{3,1}... | collective-permute-start | bytes 393224 | tf_op jit(solution)/shard_map/ppermute | solution.py:285
  99.6 3.4 %collective-permute-done.30.refs_5_ = bf16[256,256]{1,0:T(8,128)(2,1)S(1)} collective-permute-done((bf16[256,256]{1,0:T(8,128)(2,1)S(1)}, bf16[256,256]{1,0:T(8,128)(2,1)S(1)}, u32[]{:S(2)}, u32[]{:S(2)}) %collective-permute-start.30) | collective-permute-done | bytes 131104 | tf_op jit(solution)/shard_map/ppermute | solution.py:285
  103.0 0.8 collective-permute-done.32
  103.8 1.2 columns_other.1
  105.0 10.2 %collective-permute-start.33 = (bf16[4,512,128]{2,1,0:T(8,128)(2,1)S(1)}, bf16[4,512,128]{2,1,0:T(8,128)(2,1)S(1)}, u32[]{:S(2)}, u32[]{:S(2)}) collective-permute-start(bf16[4,512,128]{2,1,0:T(8,128)(2,1)S(1)} %columns_other.1), channel_id=1, source_target_pairs={{0,16},{16,0},{32,48},{48,32},{64,80},{80,64},{96,112},{112,96},{1... | collective-permute-start | bytes 1572872 | tf_op jit(solution)/shard_map/ppermute | solution.py:270
  115.2 0.9 collective-permute-start.34
  116.1 4.1 %columns_rest.1 = bf16[12,512,128]{2,1,0:T(8,128)(2,1)S(1)} custom-call(bf16[2048,2048]{1,0:T(8,128)(2,1)S(1)} %dense_build.1.refs_0_, bf16[512,256]{1,0:T(8,128)(2,1)S(1)} %get-tuple-element.104.refs_1_, bf16[512,256]{1,0:T(8,128)(2,1)S(1)} %collective-permute-done.19.refs_2_, bf16[512,256]{1,0:T(8,128)(2,1)S(1)} %collective-permute-done.22.refs_3_, ...), custom_call_target="tpu_custom_call" | custom-call | flops 3221225472 | bytes 6291456 | tf_op jit(solution)/shard_map/columns_rest/pallas_call | solution.py:144
  120.2 3.9 %collective-permute-done.34 = bf16[128,512]{1,0:T(8,128)(2,1)S(1)} collective-permute-done((bf16[128,512]{1,0:T(8,128)(2,1)S(1)}, bf16[128,512]{1,0:T(8,128)(2,1)S(1)}, u32[]{:S(2)}, u32[]{:S(2)}) %collective-permute-start.34) | collective-permute-done | bytes 131104 | tf_op jit(solution)/shard_map/ppermute | solution.py:289
  124.9 0.7 collective-permute-start.38
  125.7 3.4 %collective-permute-start.39 = (bf16[128,512]{1,0:T(8,128)(2,1)S(1)}, bf16[128,512]{1,0:T(8,128)(2,1)S(1)}, u32[]{:S(2)}, u32[]{:S(2)}) collective-permute-start(bf16[128,512]{1,0:T(8,128)(2,1)S(1)} %add_convert_fusion.8), channel_id=1, source_target_pairs={{0,8},{2,10},{4,12},{6,14},{8,0},{10,2},{12,4},{14,6},{1,9},{3,11}... | collective-permute-start | bytes 393224 | tf_op jit(solution)/shard_map/ppermute | solution.py:289
  129.0 1.7 %collective-permute-start.37 = (bf16[512,128]{1,0:T(8,128)(2,1)S(1)}, bf16[512,128]{1,0:T(8,128)(2,1)S(1)}, u32[]{:S(2)}, u32[]{:S(2)}) collective-permute-start(bf16[512,128]{1,0:T(8,128)(2,1)S(1)} %get-tuple-element.163), channel_id=1, source_target_pairs={{0,96},{16,112},{32,0},{48,16},{64,32},{80,48},{96,64},{112,80},{1... | collective-permute-start | bytes 393224 | tf_op jit(solution)/shard_map/ppermute | solution.py:281
  130.8 6.9 %collective-permute-done.39 = bf16[128,512]{1,0:T(8,128)(2,1)S(1)} collective-permute-done((bf16[128,512]{1,0:T(8,128)(2,1)S(1)}, bf16[128,512]{1,0:T(8,128)(2,1)S(1)}, u32[]{:S(2)}, u32[]{:S(2)}) %collective-permute-start.39) | collective-permute-done | bytes 131104 | tf_op jit(solution)/shard_map/ppermute | solution.py:289
  138.0 1.3 collective-permute-start.46
  139.3 0.8 collective-permute-start.45
  140.2 2.6 %collective-permute-start.40 = (bf16[512,128]{1,0:T(8,128)(2,1)S(1)}, bf16[512,128]{1,0:T(8,128)(2,1)S(1)}, u32[]{:S(2)}, u32[]{:S(2)}) collective-permute-start(bf16[512,128]{1,0:T(8,128)(2,1)S(1)} %get-tuple-element.146), channel_id=1, source_target_pairs={{0,128},{16,144},{32,160},{48,176},{64,192},{80,208},{96,224},{112... | collective-permute-start | bytes 393224 | tf_op jit(solution)/shard_map/ppermute | solution.py:270
  143.1 1.0 collective-permute-done.46.refs_4_
  144.2 1.7 %collective-permute-start.42 = (bf16[512,128]{1,0:T(8,128)(2,1)S(1)}, bf16[512,128]{1,0:T(8,128)(2,1)S(1)}, u32[]{:S(2)}, u32[]{:S(2)}) collective-permute-start(bf16[512,128]{1,0:T(8,128)(2,1)S(1)} %get-tuple-element.148), channel_id=1, source_target_pairs={{0,96},{16,112},{32,0},{48,16},{64,32},{80,48},{96,64},{112,80},{1... | collective-permute-start | bytes 393224 | tf_op jit(solution)/shard_map/ppermute | solution.py:281
  145.9 1.1 collective-permute-done.45.refs_3_
  147.4 1.6 %weight_place.1 = f32[512,512]{1,0:T(8,128)} custom-call(s32[2]{0:T(128)S(1)} %pad_add_fusion.1.where_ref.refs_0_, bf16[128,512]{1,0:T(8,128)(2,1)S(1)} %add_convert_fusion.6.refs_1_, bf16[128,512]{1,0:T(8,128)(2,1)S(1)} %collective-permute-done.44.refs_2_, bf16[128,512]{1,0:T(8,128)(2,1)S(1)} %collective-permute-done.45.refs_3_, ...), custom_call_target="tpu_custom_call" | custom-call | tf_op jit(solution)/shard_map/weight_place/pallas_call | solution.py:259
  149.0 2.6 %collective-permute-done.40.refs_1_ = bf16[512,128]{1,0:T(8,128)(2,1)S(1)} collective-permute-done((bf16[512,128]{1,0:T(8,128)(2,1)S(1)}, bf16[512,128]{1,0:T(8,128)(2,1)S(1)}, u32[]{:S(2)}, u32[]{:S(2)}) %collective-permute-start.40) | collective-permute-done | bytes 131104 | tf_op jit(solution)/shard_map/ppermute | solution.py:270
  151.5 0.8 finish.1
  (79 shorter events, 5.5 us)
Async XLA Ops:
  0.6 8.1 %collective-permute-start.3 = (bf16[128,512]{1,0:T(8,128)(2,1)}, bf16[128,512]{1,0:T(8,128)(2,1)S(1)}, u32[]{:S(2)}, u32[]{:S(2)}) collective-permute-start(bf16[128,512]{1,0:T(8,128)(2,1)} %refs_8_.3), channel_id=1, source_target_pairs={{0,16},{16,0},{32,48},{48,32},{64,80},{80,64},{96,112},{112,96},{1... | collective-permute-start | bytes 393224 | tf_op jit(solution)/shard_map/ppermute | solution.py:270
  4.0 5.3 %collective-permute-start.2 = (bf16[128,512]{1,0:T(8,128)(2,1)}, bf16[128,512]{1,0:T(8,128)(2,1)S(1)}, u32[]{:S(2)}, u32[]{:S(2)}) collective-permute-start(bf16[128,512]{1,0:T(8,128)(2,1)} %refs_8_.3), channel_id=1, source_target_pairs={{0,96},{16,112},{32,0},{48,16},{64,32},{80,48},{96,64},{112,80},{1... | collective-permute-start | bytes 393224 | tf_op jit(solution)/shard_map/ppermute | solution.py:281
  4.7 6.1 %collective-permute-start.1 = (bf16[128,512]{1,0:T(8,128)(2,1)}, bf16[128,512]{1,0:T(8,128)(2,1)S(1)}, u32[]{:S(2)}, u32[]{:S(2)}) collective-permute-start(bf16[128,512]{1,0:T(8,128)(2,1)} %refs_8_.3), channel_id=1, source_target_pairs={{0,32},{16,48},{32,64},{48,80},{64,96},{80,112},{96,0},{112,16},{1... | collective-permute-start | bytes 393224 | tf_op jit(solution)/shard_map/ppermute | solution.py:281
  5.4 6.1 %collective-permute-start = (bf16[128,512]{1,0:T(8,128)(2,1)}, bf16[128,512]{1,0:T(8,128)(2,1)S(1)}, u32[]{:S(2)}, u32[]{:S(2)}) collective-permute-start(bf16[128,512]{1,0:T(8,128)(2,1)} %refs_8_.3), channel_id=1, source_target_pairs={{0,128},{16,144},{32,160},{48,176},{64,192},{80,208},{96,224},{112... | collective-permute-start | bytes 393224 | tf_op jit(solution)/shard_map/ppermute | solution.py:270
  11.6 13.6 %collective-permute-start.7 = (bf16[384,512]{1,0:T(8,128)(2,1)S(1)}, bf16[384,512]{1,0:T(8,128)(2,1)S(1)}, u32[]{:S(2)}, u32[]{:S(2)}) collective-permute-start(bf16[384,512]{1,0:T(8,128)(2,1)S(1)} %pad_maximum_fusion), channel_id=1, source_target_pairs={{0,16},{16,0},{32,48},{48,32},{64,80},{80,64},{96,112},{112,96},{1... | collective-permute-start | bytes 1179656 | tf_op jit(solution)/shard_map/ppermute | solution.py:270
  13.2 12.0 %collective-permute-start.4 = (bf16[256,512]{1,0:T(8,128)(2,1)S(1)}, bf16[256,512]{1,0:T(8,128)(2,1)S(1)}, u32[]{:S(2)}, u32[]{:S(2)}) collective-permute-start(bf16[256,512]{1,0:T(8,128)(2,1)S(1)} %pad_maximum_fusion.1), channel_id=1, source_target_pairs={{0,128},{16,144},{32,160},{48,176},{64,192},{80,208},{96,224},{112... | collective-permute-start | bytes 786440 | tf_op jit(solution)/shard_map/ppermute | solution.py:270
  15.5 9.7 %collective-permute-start.6 = (bf16[128,512]{1,0:T(8,128)(2,1)S(1)}, bf16[128,512]{1,0:T(8,128)(2,1)S(1)}, u32[]{:S(2)}, u32[]{:S(2)}) collective-permute-start(bf16[128,512]{1,0:T(8,128)(2,1)S(1)} %collective-permute-done.refs_4_), channel_id=1, source_target_pairs={{0,64},{16,80},{32,96},{48,112},{64,0},{80,16},{96,32},{112,48},{1... | collective-permute-start | bytes 393224 | tf_op jit(solution)/shard_map/ppermute | solution.py:270
  17.2 8.0 %collective-permute-start.5 = (bf16[128,512]{1,0:T(8,128)(2,1)S(1)}, bf16[128,512]{1,0:T(8,128)(2,1)S(1)}, u32[]{:S(2)}, u32[]{:S(2)}) collective-permute-start(bf16[128,512]{1,0:T(8,128)(2,1)S(1)} %collective-permute-done.1.refs_6_), channel_id=1, source_target_pairs={{0,32},{16,48},{32,64},{48,80},{64,96},{80,112},{96,0},{112,16},{1... | collective-permute-start | bytes 393224 | tf_op jit(solution)/shard_map/ppermute | solution.py:281
  19.4 2.2 %copy-start = (bf16[128,128,128]{2,1,0:T(8,128)(2,1)S(1)}, bf16[128,128,128]{2,1,0:T(8,128)(2,1)}, u32[]{:S(2)}) copy-start(bf16[128,128,128]{2,1,0:T(8,128)(2,1)} %tiles_ref.1) | copy-start | bytes 12582916
  21.6 4.6 %copy-start.3 = (bf16[128,512]{1,0:T(8,128)(2,1)S(1)}, bf16[128,512]{1,0:T(8,128)(2,1)}, u32[]{:S(2)}) copy-start(bf16[128,512]{1,0:T(8,128)(2,1)} %cot_ref.1) | copy-start | bytes 393220
  21.6 6.1 %copy-start.2 = (bf16[128,512]{1,0:T(8,128)(2,1)S(1)}, bf16[128,512]{1,0:T(8,128)(2,1)}, u32[]{:S(2)}) copy-start(bf16[128,512]{1,0:T(8,128)(2,1)} %refs_8_.3) | copy-start | bytes 393220
  25.3 2.4 %collective-permute-start.8 = (bf16[512,512]{1,0:T(8,128)(2,1)S(1)}, bf16[512,512]{1,0:T(8,128)(2,1)S(1)}, u32[]{:S(2)}, u32[]{:S(2)}) collective-permute-start(bf16[512,512]{1,0:T(8,128)(2,1)S(1)} %constant_dynamic-update-slice_fusion.refs_2_), channel_id=1, source_target_pairs={{0,16},{16,0},{32,48},{48,32},{64,80},{80,64},{96,112},{112,96},{1... | collective-permute-start | bytes 1572872 | tf_op jit(solution)/shard_map/ppermute | solution.py:270
  26.1 13.1 %collective-permute-start.11 = (bf16[128,512]{1,0:T(8,128)(2,1)S(1)}, bf16[128,512]{1,0:T(8,128)(2,1)S(1)}, u32[]{:S(2)}, u32[]{:S(2)}) collective-permute-start(bf16[128,512]{1,0:T(8,128)(2,1)S(1)} %copy-done.3), channel_id=1, source_target_pairs={{0,1},{1,0},{2,3},{3,2},{4,5},{5,4},{6,7},{7,6},{8,9},{9,8},{10,11... | collective-permute-start | bytes 393224 | tf_op jit(solution)/shard_map/ppermute | solution.py:293
  28.4 10.7 %collective-permute-start.9 = (bf16[128,512]{1,0:T(8,128)(2,1)S(1)}, bf16[128,512]{1,0:T(8,128)(2,1)S(1)}, u32[]{:S(2)}, u32[]{:S(2)}) collective-permute-start(bf16[128,512]{1,0:T(8,128)(2,1)S(1)} %get-tuple-element.87), channel_id=1, source_target_pairs={{0,2},{2,4},{4,6},{6,8},{8,10},{10,12},{12,14},{14,0},{1,3},{3,5},... | collective-permute-start | bytes 393224 | tf_op jit(solution)/shard_map/ppermute | solution.py:285
  30.1 9.0 %collective-permute-start.10 = (bf16[128,512]{1,0:T(8,128)(2,1)S(1)}, bf16[128,512]{1,0:T(8,128)(2,1)S(1)}, u32[]{:S(2)}, u32[]{:S(2)}) collective-permute-start(bf16[128,512]{1,0:T(8,128)(2,1)S(1)} %get-tuple-element.88), channel_id=1, source_target_pairs={{0,14},{2,0},{4,2},{6,4},{8,6},{10,8},{12,10},{14,12},{1,15},{3,1}... | collective-permute-start | bytes 393224 | tf_op jit(solution)/shard_map/ppermute | solution.py:285
  39.3 28.7 %copy-start.1 = (bf16[512,512]{1,0:T(8,128)(2,1)S(1)}, bf16[512,512]{1,0:T(8,128)(2,1)}, u32[]{:S(2)}) copy-start(bf16[512,512]{1,0:T(8,128)(2,1)} %weight_ref.1) | copy-start | bytes 1572868
  39.3 8.5 %collective-permute-start.12 = (bf16[256,512]{1,0:T(8,128)(2,1)S(1)}, bf16[256,512]{1,0:T(8,128)(2,1)S(1)}, u32[]{:S(2)}, u32[]{:S(2)}) collective-permute-start(bf16[256,512]{1,0:T(8,128)(2,1)S(1)} %get-tuple-element.89), channel_id=1, source_target_pairs={{0,2},{2,4},{4,6},{6,8},{8,10},{10,12},{12,14},{14,0},{1,3},{3,5},... | collective-permute-start | bytes 786440 | tf_op jit(solution)/shard_map/ppermute | solution.py:285
  39.4 8.4 %collective-permute-start.13 = (bf16[256,512]{1,0:T(8,128)(2,1)S(1)}, bf16[256,512]{1,0:T(8,128)(2,1)S(1)}, u32[]{:S(2)}, u32[]{:S(2)}) collective-permute-start(bf16[256,512]{1,0:T(8,128)(2,1)S(1)} %get-tuple-element.90), channel_id=1, source_target_pairs={{0,14},{2,0},{4,2},{6,4},{8,6},{10,8},{12,10},{14,12},{1,15},{3,1}... | collective-permute-start | bytes 786440 | tf_op jit(solution)/shard_map/ppermute | solution.py:285
  47.9 7.6 %collective-permute-start.14 = (bf16[256,512]{1,0:T(8,128)(2,1)S(1)}, bf16[256,512]{1,0:T(8,128)(2,1)S(1)}, u32[]{:S(2)}, u32[]{:S(2)}) collective-permute-start(bf16[256,512]{1,0:T(8,128)(2,1)S(1)} %get-tuple-element.93), channel_id=1, source_target_pairs={{0,2},{2,4},{4,6},{6,8},{8,10},{10,12},{12,14},{14,0},{1,3},{3,5},... | collective-permute-start | bytes 786440 | tf_op jit(solution)/shard_map/ppermute | solution.py:285
  48.0 7.5 %collective-permute-start.15 = (bf16[256,512]{1,0:T(8,128)(2,1)S(1)}, bf16[256,512]{1,0:T(8,128)(2,1)S(1)}, u32[]{:S(2)}, u32[]{:S(2)}) collective-permute-start(bf16[256,512]{1,0:T(8,128)(2,1)S(1)} %get-tuple-element.94), channel_id=1, source_target_pairs={{0,14},{2,0},{4,2},{6,4},{8,6},{10,8},{12,10},{14,12},{1,15},{3,1}... | collective-permute-start | bytes 786440 | tf_op jit(solution)/shard_map/ppermute | solution.py:285
  55.6 6.5 %collective-permute-start.16 = (bf16[256,512]{1,0:T(8,128)(2,1)S(1)}, bf16[256,512]{1,0:T(8,128)(2,1)S(1)}, u32[]{:S(2)}, u32[]{:S(2)}) collective-permute-start(bf16[256,512]{1,0:T(8,128)(2,1)S(1)} %get-tuple-element.97), channel_id=1, source_target_pairs={{0,2},{2,4},{4,6},{6,8},{8,10},{10,12},{12,14},{14,0},{1,3},{3,5},... | collective-permute-start | bytes 786440 | tf_op jit(solution)/shard_map/ppermute | solution.py:285
  57.0 5.5 %collective-permute-start.17 = (bf16[256,512]{1,0:T(8,128)(2,1)S(1)}, bf16[256,512]{1,0:T(8,128)(2,1)S(1)}, u32[]{:S(2)}, u32[]{:S(2)}) collective-permute-start(bf16[256,512]{1,0:T(8,128)(2,1)S(1)} %get-tuple-element.98), channel_id=1, source_target_pairs={{0,14},{2,0},{4,2},{6,4},{8,6},{10,8},{12,10},{14,12},{1,15},{3,1}... | collective-permute-start | bytes 786440 | tf_op jit(solution)/shard_map/ppermute | solution.py:285
  62.6 5.3 %collective-permute-start.18 = (bf16[256,512]{1,0:T(8,128)(2,1)S(1)}, bf16[256,512]{1,0:T(8,128)(2,1)S(1)}, u32[]{:S(2)}, u32[]{:S(2)}) collective-permute-start(bf16[256,512]{1,0:T(8,128)(2,1)S(1)} %add_convert_fusion.1.mine_ref), channel_id=1, source_target_pairs={{0,1},{1,0},{2,3},{3,2},{4,5},{5,4},{6,7},{7,6},{8,9},{9,8},{10,11... | collective-permute-start | bytes 786440 | tf_op jit(solution)/shard_map/ppermute | solution.py:293
  68.9 10.4 %collective-permute-start.20 = (bf16[512,256]{1,0:T(8,128)(2,1)S(1)}, bf16[512,256]{1,0:T(8,128)(2,1)S(1)}, u32[]{:S(2)}, u32[]{:S(2)}) collective-permute-start(bf16[512,256]{1,0:T(8,128)(2,1)S(1)} %get-tuple-element.104.refs_1_), channel_id=1, source_target_pairs={{0,2},{2,4},{4,6},{6,8},{8,10},{10,12},{12,14},{14,0},{1,3},{3,5},... | collective-permute-start | bytes 786440 | tf_op jit(solution)/shard_map/ppermute | solution.py:285
  70.5 8.9 %collective-permute-start.19 = (bf16[512,256]{1,0:T(8,128)(2,1)S(1)}, bf16[512,256]{1,0:T(8,128)(2,1)S(1)}, u32[]{:S(2)}, u32[]{:S(2)}) collective-permute-start(bf16[512,256]{1,0:T(8,128)(2,1)S(1)} %get-tuple-element.104.refs_1_), channel_id=1, source_target_pairs={{0,14},{2,0},{4,2},{6,4},{8,6},{10,8},{12,10},{14,12},{1,15},{3,1}... | collective-permute-start | bytes 786440 | tf_op jit(solution)/shard_map/ppermute | solution.py:285
  72.4 7.0 %collective-permute-start.21 = (bf16[128,512]{1,0:T(8,128)(2,1)S(1)}, bf16[128,512]{1,0:T(8,128)(2,1)S(1)}, u32[]{:S(2)}, u32[]{:S(2)}) collective-permute-start(bf16[128,512]{1,0:T(8,128)(2,1)S(1)} %get-tuple-element.108), channel_id=1, source_target_pairs={{0,16},{16,0},{32,48},{48,32},{64,80},{80,64},{96,112},{112,96},{1... | collective-permute-start | bytes 393224 | tf_op jit(solution)/shard_map/ppermute | solution.py:270
  79.4 8.9 %collective-permute-start.22 = (bf16[512,256]{1,0:T(8,128)(2,1)S(1)}, bf16[512,256]{1,0:T(8,128)(2,1)S(1)}, u32[]{:S(2)}, u32[]{:S(2)}) collective-permute-start(bf16[512,256]{1,0:T(8,128)(2,1)S(1)} %collective-permute-done.19.refs_2_), channel_id=1, source_target_pairs={{0,14},{2,0},{4,2},{6,4},{8,6},{10,8},{12,10},{14,12},{1,15},{3,1}... | collective-permute-start | bytes 786440 | tf_op jit(solution)/shard_map/ppermute | solution.py:285
  80.2 8.0 %collective-permute-start.23 = (bf16[512,256]{1,0:T(8,128)(2,1)S(1)}, bf16[512,256]{1,0:T(8,128)(2,1)S(1)}, u32[]{:S(2)}, u32[]{:S(2)}) collective-permute-start(bf16[512,256]{1,0:T(8,128)(2,1)S(1)} %collective-permute-done.20.refs_9_), channel_id=1, source_target_pairs={{0,2},{2,4},{4,6},{6,8},{8,10},{10,12},{12,14},{14,0},{1,3},{3,5},... | collective-permute-start | bytes 786440 | tf_op jit(solution)/shard_map/ppermute | solution.py:285
  81.0 6.4 %collective-permute-start.26 = (bf16[128,512]{1,0:T(8,128)(2,1)S(1)}, bf16[128,512]{1,0:T(8,128)(2,1)S(1)}, u32[]{:S(2)}, u32[]{:S(2)}) collective-permute-start(bf16[128,512]{1,0:T(8,128)(2,1)S(1)} %add_convert_fusion.12), channel_id=1, source_target_pairs={{0,96},{16,112},{32,64},{48,80},{64,32},{80,48},{96,0},{112,16},{1... | collective-permute-start | bytes 393224 | tf_op jit(solution)/shard_map/ppermute | solution.py:270
  81.7 5.7 %collective-permute-start.25 = (bf16[128,512]{1,0:T(8,128)(2,1)S(1)}, bf16[128,512]{1,0:T(8,128)(2,1)S(1)}, u32[]{:S(2)}, u32[]{:S(2)}) collective-permute-start(bf16[128,512]{1,0:T(8,128)(2,1)S(1)} %add_convert_fusion.12), channel_id=1, source_target_pairs={{0,64},{16,80},{32,96},{48,112},{64,0},{80,16},{96,32},{112,48},{1... | collective-permute-start | bytes 393224 | tf_op jit(solution)/shard_map/ppermute | solution.py:270
  82.5 5.8 %collective-permute-start.24 = (bf16[128,512]{1,0:T(8,128)(2,1)S(1)}, bf16[128,512]{1,0:T(8,128)(2,1)S(1)}, u32[]{:S(2)}, u32[]{:S(2)}) collective-permute-start(bf16[128,512]{1,0:T(8,128)(2,1)S(1)} %add_convert_fusion.12), channel_id=1, source_target_pairs={{0,32},{16,48},{32,0},{48,16},{64,96},{80,112},{96,64},{112,80},{1... | collective-permute-start | bytes 393224 | tf_op jit(solution)/shard_map/ppermute | solution.py:270
  88.4 7.4 %collective-permute-start.27 = (bf16[512,256]{1,0:T(8,128)(2,1)S(1)}, bf16[512,256]{1,0:T(8,128)(2,1)S(1)}, u32[]{:S(2)}, u32[]{:S(2)}) collective-permute-start(bf16[512,256]{1,0:T(8,128)(2,1)S(1)} %collective-permute-done.22.refs_3_), channel_id=1, source_target_pairs={{0,14},{2,0},{4,2},{6,4},{8,6},{10,8},{12,10},{14,12},{1,15},{3,1}... | collective-permute-start | bytes 786440 | tf_op jit(solution)/shard_map/ppermute | solution.py:285
  90.4 6.4 %collective-permute-start.28 = (bf16[512,256]{1,0:T(8,128)(2,1)S(1)}, bf16[512,256]{1,0:T(8,128)(2,1)S(1)}, u32[]{:S(2)}, u32[]{:S(2)}) collective-permute-start(bf16[512,256]{1,0:T(8,128)(2,1)S(1)} %collective-permute-done.23.refs_8_), channel_id=1, source_target_pairs={{0,2},{2,4},{4,6},{6,8},{8,10},{10,12},{12,14},{14,0},{1,3},{3,5},... | collective-permute-start | bytes 786440 | tf_op jit(solution)/shard_map/ppermute | solution.py:285
  90.4 5.3 %collective-permute-start.29 = (bf16[128,512]{1,0:T(8,128)(2,1)S(1)}, bf16[128,512]{1,0:T(8,128)(2,1)S(1)}, u32[]{:S(2)}, u32[]{:S(2)}) collective-permute-start(bf16[128,512]{1,0:T(8,128)(2,1)S(1)} %add_convert_fusion.11), channel_id=1, source_target_pairs={{0,128},{16,144},{32,160},{48,176},{64,192},{80,208},{96,224},{112... | collective-permute-start | bytes 393224 | tf_op jit(solution)/shard_map/ppermute | solution.py:270
  96.9 6.1 %collective-permute-start.30 = (bf16[256,256]{1,0:T(8,128)(2,1)S(1)}, bf16[256,256]{1,0:T(8,128)(2,1)S(1)}, u32[]{:S(2)}, u32[]{:S(2)}) collective-permute-start(bf16[256,256]{1,0:T(8,128)(2,1)S(1)} %slice.109), channel_id=1, source_target_pairs={{0,2},{2,4},{4,6},{6,8},{8,10},{10,12},{12,14},{14,0},{1,3},{3,5},... | collective-permute-start | bytes 393224 | tf_op jit(solution)/shard_map/ppermute | solution.py:285
  97.0 6.0 %collective-permute-start.31 = (bf16[256,256]{1,0:T(8,128)(2,1)S(1)}, bf16[256,256]{1,0:T(8,128)(2,1)S(1)}, u32[]{:S(2)}, u32[]{:S(2)}) collective-permute-start(bf16[256,256]{1,0:T(8,128)(2,1)S(1)} %slice.110), channel_id=1, source_target_pairs={{0,14},{2,0},{4,2},{6,4},{8,6},{10,8},{12,10},{14,12},{1,15},{3,1}... | collective-permute-start | bytes 393224 | tf_op jit(solution)/shard_map/ppermute | solution.py:285
  99.6 4.1 %collective-permute-start.32 = (bf16[128,512]{1,0:T(8,128)(2,1)S(1)}, bf16[128,512]{1,0:T(8,128)(2,1)S(1)}, u32[]{:S(2)}, u32[]{:S(2)}) collective-permute-start(bf16[128,512]{1,0:T(8,128)(2,1)S(1)} %add_convert_fusion.10), channel_id=1, source_target_pairs={{0,2},{2,0},{4,6},{6,4},{8,10},{10,8},{12,14},{14,12},{1,3},{3,1},... | collective-permute-start | bytes 393224 | tf_op jit(solution)/shard_map/ppermute | solution.py:289
  105.0 19.1 %collective-permute-start.33 = (bf16[4,512,128]{2,1,0:T(8,128)(2,1)S(1)}, bf16[4,512,128]{2,1,0:T(8,128)(2,1)S(1)}, u32[]{:S(2)}, u32[]{:S(2)}) collective-permute-start(bf16[4,512,128]{2,1,0:T(8,128)(2,1)S(1)} %columns_other.1), channel_id=1, source_target_pairs={{0,16},{16,0},{32,48},{48,32},{64,80},{80,64},{96,112},{112,96},{1... | collective-permute-start | bytes 1572872 | tf_op jit(solution)/shard_map/ppermute | solution.py:270
  115.2 9.0 %collective-permute-start.34 = (bf16[128,512]{1,0:T(8,128)(2,1)S(1)}, bf16[128,512]{1,0:T(8,128)(2,1)S(1)}, u32[]{:S(2)}, u32[]{:S(2)}) collective-permute-start(bf16[128,512]{1,0:T(8,128)(2,1)S(1)} %add_convert_fusion.9), channel_id=1, source_target_pairs={{0,4},{2,6},{4,0},{6,2},{8,12},{10,14},{12,8},{14,10},{1,5},{3,7},... | collective-permute-start | bytes 393224 | tf_op jit(solution)/shard_map/ppermute | solution.py:289
  124.4 13.3 %collective-permute-start.35 = (bf16[2,512,128]{2,1,0:T(8,128)(2,1)S(1)}, bf16[2,512,128]{2,1,0:T(8,128)(2,1)S(1)}, u32[]{:S(2)}, u32[]{:S(2)}) collective-permute-start(bf16[2,512,128]{2,1,0:T(8,128)(2,1)S(1)} %slice.115), channel_id=1, source_target_pairs={{0,128},{16,144},{32,160},{48,176},{64,192},{80,208},{96,224},{112... | collective-permute-start | bytes 786440 | tf_op jit(solution)/shard_map/ppermute | solution.py:270
  124.9 12.8 %collective-permute-start.38 = (bf16[3,512,128]{2,1,0:T(8,128)(2,1)S(1)}, bf16[3,512,128]{2,1,0:T(8,128)(2,1)S(1)}, u32[]{:S(2)}, u32[]{:S(2)}) collective-permute-start(bf16[3,512,128]{2,1,0:T(8,128)(2,1)S(1)} %slice.114), channel_id=1, source_target_pairs={{0,16},{16,0},{32,48},{48,32},{64,80},{80,64},{96,112},{112,96},{1... | collective-permute-start | bytes 1179656 | tf_op jit(solution)/shard_map/ppermute | solution.py:270
  125.7 12.0 %collective-permute-start.39 = (bf16[128,512]{1,0:T(8,128)(2,1)S(1)}, bf16[128,512]{1,0:T(8,128)(2,1)S(1)}, u32[]{:S(2)}, u32[]{:S(2)}) collective-permute-start(bf16[128,512]{1,0:T(8,128)(2,1)S(1)} %add_convert_fusion.8), channel_id=1, source_target_pairs={{0,8},{2,10},{4,12},{6,14},{8,0},{10,2},{12,4},{14,6},{1,9},{3,11}... | collective-permute-start | bytes 393224 | tf_op jit(solution)/shard_map/ppermute | solution.py:289
  129.0 8.7 %collective-permute-start.37 = (bf16[512,128]{1,0:T(8,128)(2,1)S(1)}, bf16[512,128]{1,0:T(8,128)(2,1)S(1)}, u32[]{:S(2)}, u32[]{:S(2)}) collective-permute-start(bf16[512,128]{1,0:T(8,128)(2,1)S(1)} %get-tuple-element.163), channel_id=1, source_target_pairs={{0,96},{16,112},{32,0},{48,16},{64,32},{80,48},{96,64},{112,80},{1... | collective-permute-start | bytes 393224 | tf_op jit(solution)/shard_map/ppermute | solution.py:281
  130.7 7.0 %collective-permute-start.36 = (bf16[512,128]{1,0:T(8,128)(2,1)S(1)}, bf16[512,128]{1,0:T(8,128)(2,1)S(1)}, u32[]{:S(2)}, u32[]{:S(2)}) collective-permute-start(bf16[512,128]{1,0:T(8,128)(2,1)S(1)} %get-tuple-element.164), channel_id=1, source_target_pairs={{0,64},{16,80},{32,96},{48,112},{64,0},{80,16},{96,32},{112,48},{1... | collective-permute-start | bytes 393224 | tf_op jit(solution)/shard_map/ppermute | solution.py:270
  138.0 6.2 %collective-permute-start.46 = (bf16[128,512]{1,0:T(8,128)(2,1)S(1)}, bf16[128,512]{1,0:T(8,128)(2,1)S(1)}, u32[]{:S(2)}, u32[]{:S(2)}) collective-permute-start(bf16[128,512]{1,0:T(8,128)(2,1)S(1)} %add_convert_fusion.6.refs_1_), channel_id=1, source_target_pairs={{0,17},{1,16},{16,1},{17,0},{32,49},{33,48},{48,33},{49,32},{64,81... | collective-permute-start | bytes 393224 | tf_op jit(solution)/shard_map/ppermute | solution.py:298
  139.3 7.6 %collective-permute-start.45 = (bf16[128,512]{1,0:T(8,128)(2,1)S(1)}, bf16[128,512]{1,0:T(8,128)(2,1)S(1)}, u32[]{:S(2)}, u32[]{:S(2)}) collective-permute-start(bf16[128,512]{1,0:T(8,128)(2,1)S(1)} %add_convert_fusion.6.refs_1_), channel_id=1, source_target_pairs={{0,1},{1,0},{2,3},{3,2},{4,5},{5,4},{6,7},{7,6},{8,9},{9,8},{10,11... | collective-permute-start | bytes 393224 | tf_op jit(solution)/shard_map/ppermute | solution.py:293
  140.1 7.3 %collective-permute-start.44 = (bf16[128,512]{1,0:T(8,128)(2,1)S(1)}, bf16[128,512]{1,0:T(8,128)(2,1)S(1)}, u32[]{:S(2)}, u32[]{:S(2)}) collective-permute-start(bf16[128,512]{1,0:T(8,128)(2,1)S(1)} %add_convert_fusion.6.refs_1_), channel_id=1, source_target_pairs={{0,16},{16,0},{32,48},{48,32},{64,80},{80,64},{96,112},{112,96},{1... | collective-permute-start | bytes 393224 | tf_op jit(solution)/shard_map/ppermute | solution.py:270
  140.2 11.3 %collective-permute-start.40 = (bf16[512,128]{1,0:T(8,128)(2,1)S(1)}, bf16[512,128]{1,0:T(8,128)(2,1)S(1)}, u32[]{:S(2)}, u32[]{:S(2)}) collective-permute-start(bf16[512,128]{1,0:T(8,128)(2,1)S(1)} %get-tuple-element.146), channel_id=1, source_target_pairs={{0,128},{16,144},{32,160},{48,176},{64,192},{80,208},{96,224},{112... | collective-permute-start | bytes 393224 | tf_op jit(solution)/shard_map/ppermute | solution.py:270
  142.8 8.8 %collective-permute-start.41 = (bf16[512,128]{1,0:T(8,128)(2,1)S(1)}, bf16[512,128]{1,0:T(8,128)(2,1)S(1)}, u32[]{:S(2)}, u32[]{:S(2)}) collective-permute-start(bf16[512,128]{1,0:T(8,128)(2,1)S(1)} %fusion.2), channel_id=1, source_target_pairs={{0,32},{16,48},{32,64},{48,80},{64,96},{80,112},{96,0},{112,16},{1... | collective-permute-start | bytes 393224 | tf_op jit(solution)/shard_map/ppermute | solution.py:281
  144.2 7.4 %collective-permute-start.42 = (bf16[512,128]{1,0:T(8,128)(2,1)S(1)}, bf16[512,128]{1,0:T(8,128)(2,1)S(1)}, u32[]{:S(2)}, u32[]{:S(2)}) collective-permute-start(bf16[512,128]{1,0:T(8,128)(2,1)S(1)} %get-tuple-element.148), channel_id=1, source_target_pairs={{0,96},{16,112},{32,0},{48,16},{64,32},{80,48},{96,64},{112,80},{1... | collective-permute-start | bytes 393224 | tf_op jit(solution)/shard_map/ppermute | solution.py:281
  147.0 4.6 %collective-permute-start.43 = (bf16[512,128]{1,0:T(8,128)(2,1)S(1)}, bf16[512,128]{1,0:T(8,128)(2,1)S(1)}, u32[]{:S(2)}, u32[]{:S(2)}) collective-permute-start(bf16[512,128]{1,0:T(8,128)(2,1)S(1)} %get-tuple-element.149), channel_id=1, source_target_pairs={{0,16},{16,0},{32,48},{48,32},{64,80},{80,64},{96,112},{112,96},{1... | collective-permute-start | bytes 393224 | tf_op jit(solution)/shard_map/ppermute | solution.py:270
where the time goes:
time: 152 us
  starting transfers between devices  73 us (48%)
  waiting for transfers between devices  54.2 us (36%)
  Pallas kernels  18.9 us (12%)
  local copies, waits for them, and re-layouts  2.63 us (2%)
  other arithmetic  1.95 us (1%)
  between operations  1.66 us (1%)
    ppermute x18, starting transfers between devices, swap_row(): return lax.ppermute(value, 'row', [(r, r ^ mask) for r in range(16)])  36.4 us
    ppermute x16, starting transfers between devices, along_z(): return lax.ppermute(value, 'col', [(z, (z + step) % 8) for z in range(8)])  22.8 us
    ppermute x16, waiting for transfers between devices, along_z(): return lax.ppermute(value, 'col', [(z, (z + step) % 8) for z in range(8)])  19.2 us
    ppermute x18, waiting for transfers between devices, swap_row(): return lax.ppermute(value, 'row', [(r, r ^ mask) for r in range(16)])  14 us
    ppermute x3, waiting for transfers between devices, swap_z(): return lax.ppermute(value, 'col', [(z, z ^ mask) for z in range(8)])  11.6 us
    ppermute x6, starting transfers between devices, along_x(): return lax.ppermute(value, 'row', [(r, target(r)) for r in range(16)])  6.74 us
    ppermute x3, waiting for transfers between devices, swap_rep(): return lax.ppermute(value, 'rep', [(0, 1), (1, 0)])  6.3 us
    pallas_call x2, Pallas kernels, rows_dot(): pl.pallas_call(lambda *refs: rows_kernel(first, *refs), out_shape=jax.Sha...  5.78 us
  transfers between devices with their start and end apart: 47, of which 21 were waited for; matrix products, arithmetic and copies ran while one was open for 1% of the time, Pallas kernels for 10%

commit v1 on v0

--- a/solution.py
+++ b/solution.py
@@ -82,7 +82,7 @@
     )(tile_counts, places, tile_values)
 
 
-def rows_kernel(first, dense_ref, *refs):
+def rows_kernel(first, stride, dense_ref, *refs):
     pieces, (out_ref, panel_ref) = refs[:-2], refs[-2:]
     at = 0
     for piece in pieces:
@@ -90,7 +90,7 @@
         at += piece.shape[0]
 
     def product(i, carry):
-        start = pl.multiple_of((first + i * BLOCK) & (SIDE - 1), BLOCK)
+        start = pl.multiple_of((first + i * stride) & (SIDE - 1), BLOCK)
         out_ref[pl.ds(pl.multiple_of(i * BLOCK, BLOCK), BLOCK), :] = jnp.dot(
             dense_ref[pl.ds(start, BLOCK), :], panel_ref[...], preferred_element_type=F32
         ).astype(BF16)
@@ -99,10 +99,10 @@
     lax.fori_loop(0, out_ref.shape[0] // BLOCK, product, 0)
 
 
-def rows_dot(dense, pieces, first, rows, name):
+def rows_dot(dense, pieces, first, stride, rows, name):
     width = pieces[0].shape[1]
     return pl.pallas_call(
-        lambda *refs: rows_kernel(first, *refs),
+        lambda *refs: rows_kernel(first, stride, *refs),
         out_shape=jax.ShapeDtypeStruct((rows, width), BF16),
         in_specs=[WHOLE] * (1 + len(pieces)),
         out_specs=WHOLE,
@@ -346,20 +346,21 @@
     cot_twin = swap_rep(cotangent)
     pieces = (core_late, late, core_soon, half, right, left, core, features)
 
-    middle = rows_dot(dense, pieces, 1024, 256, "rows_middle")
+    middle = rows_dot(dense, pieces, 1024, 256, 256, "rows_middle")
     up, down, middle = fence(middle[:128], middle[128:], middle)
     up, down = along_z(up, 1), along_z(down, -1)
-    rest = rows_dot(dense, pieces, 1280, 1792, "rows_rest")
-
-    def block(d):
-        at = (d - 5) % 8 * 256
-        return rest[at : at + 256]
-
-    ahead, behind = block(3), block(5)
+    outer = rows_dot(dense, pieces, 768, 512, 512, "rows_outer")
+    ahead, behind = outer[:256], outer[256:]
     up = stack(wide_sum(ahead[:128], up), ahead[128:])
     down = stack(behind[:128], wide_sum(behind[128:], down))
-    up, down, cot_twin = fence(up, down, cot_twin)
+    up, down, cot_twin, core = fence(up, down, cot_twin, core)
     up, down = along_z(up, 1), along_z(down, -1)
+    inner = rows_dot(dense, pieces[:6] + (core, features), 1536, 256, 1280, "rows_inner")
+
+    def block(d):
+        at = (d - 6) % 8 * 256
+        return inner[at : at + 256]
+
     up, down = fence(up, down)
     up, down = fence(wide_sum(block(2), up), wide_sum(block(6), down))
     up, down = along_z(up, 1), along_z(down, -1)
@@ -401,7 +402,6 @@
     rows = (here, near[1], next_near[1], far[1], below, above, far[0], next_near[0], near[0])
 
     other = columns_dot(dense, rows, 0, 4, "columns_other")
-    other, share = fence(other, share)
     other = swap_core(other)
     taken = swap_z(share, 2)
     rest = columns_dot(dense, rows, 512, 12, "columns_rest")

time: 152 us -> 151 us (level)
  waiting for transfers between devices: 54.2 us -> 51.6 us
    ppermute x16, waiting for transfers between devices: 19.2 us -> 17.1 us  [along_z(): return lax.ppermute(value, 'col', [(z, (z + step) % 8) for z in range(8)])]
    pallas_call x2 -> x3, Pallas kernels: 5.78 us -> 5.92 us  [rows_dot(): pl.pallas_call(lambda *refs: rows_kernel(first, stride, *refs), out_shape...]
  transfers between devices with their start and end apart: 47 -> 47, of which waited for: 21 -> 21; matrix products, arithmetic and copies ran while one was open for 1% -> 1% of each run, Pallas kernels for 10% -> 11%
where the time goes in v1:
time: 151 us; the launch traced here: 150 us
  starting transfers between devices  73.4 us (49%)
  waiting for transfers between devices  51.6 us (34%)
  Pallas kernels  19 us (13%)
  local copies, waits for them, and re-layouts  2.63 us (2%)
  other arithmetic  1.96 us (1%)
  between operations  1.64 us (1%)
    ppermute x18, starting transfers between devices, swap_row(): return lax.ppermute(value, 'row', [(r, r ^ mask) for r in range(16)])  37.1 us
    ppermute x16, starting transfers between devices, along_z(): return lax.ppermute(value, 'col', [(z, (z + step) % 8) for z in range(8)])  23.6 us
    ppermute x16, waiting for transfers between devices, along_z(): return lax.ppermute(value, 'col', [(z, (z + step) % 8) for z in range(8)])  17.1 us
    ppermute x18, waiting for transfers between devices, swap_row(): return lax.ppermute(value, 'row', [(r, r ^ mask) for r in range(16)])  14 us
    ppermute x3, waiting for transfers between devices, swap_z(): return lax.ppermute(value, 'col', [(z, z ^ mask) for z in range(8)])  11.9 us
    ppermute x6, starting transfers between devices, along_x(): return lax.ppermute(value, 'row', [(r, target(r)) for r in range(16)])  6.73 us
    pallas_call x3, Pallas kernels, rows_dot(): pl.pallas_call(lambda *refs: rows_kernel(first, stride, *refs), out_shape...  5.92 us
    ppermute x3, waiting for transfers between devices, swap_rep(): return lax.ppermute(value, 'rep', [(0, 1), (1, 0)])  5.51 us
  transfers between devices with their start and end apart: 47, of which 21 were waited for; matrix products, arithmetic and copies ran while one was open for 1% of the time, Pallas kernels for 11%

profile of v1, /device:TPU:1, one launch (start us, length us, event | category | flops | bytes accessed | tf_op | source)
XLA Modules:
  0.0 150.2 jit_solution(4159994632888872584)
XLA Ops:
  0.6 3.3 %collective-permute-start.3 = (bf16[128,512]{1,0:T(8,128)(2,1)}, bf16[128,512]{1,0:T(8,128)(2,1)S(1)}, u32[]{:S(2)}, u32[]{:S(2)}) collective-permute-start(bf16[128,512]{1,0:T(8,128)(2,1)} %refs_8_.5), channel_id=1, source_target_pairs={{0,16},{16,0},{32,48},{48,32},{64,80},{80,64},{96,112},{112,96},{1... | collective-permute-start | bytes 393224 | tf_op jit(solution)/shard_map/ppermute | solution.py:270
  4.0 0.8 collective-permute-start.2
  4.7 0.7 collective-permute-start.1
  5.4 2.2 %collective-permute-start = (bf16[128,512]{1,0:T(8,128)(2,1)}, bf16[128,512]{1,0:T(8,128)(2,1)S(1)}, u32[]{:S(2)}, u32[]{:S(2)}) collective-permute-start(bf16[128,512]{1,0:T(8,128)(2,1)} %refs_8_.5), channel_id=1, source_target_pairs={{0,128},{16,144},{32,160},{48,176},{64,192},{80,208},{96,224},{112... | collective-permute-start | bytes 393224 | tf_op jit(solution)/shard_map/ppermute | solution.py:270
  7.6 0.8 xor_add_fusion
  9.2 1.6 %collective-permute-done.1.refs_6_ = bf16[128,512]{1,0:T(8,128)(2,1)S(1)} collective-permute-done((bf16[128,512]{1,0:T(8,128)(2,1)}, bf16[128,512]{1,0:T(8,128)(2,1)S(1)}, u32[]{:S(2)}, u32[]{:S(2)}) %collective-permute-start.1) | collective-permute-done | bytes 131104 | tf_op jit(solution)/shard_map/ppermute | solution.py:281
  11.6 1.6 %collective-permute-start.7 = (bf16[384,512]{1,0:T(8,128)(2,1)S(1)}, bf16[384,512]{1,0:T(8,128)(2,1)S(1)}, u32[]{:S(2)}, u32[]{:S(2)}) collective-permute-start(bf16[384,512]{1,0:T(8,128)(2,1)S(1)} %pad_maximum_fusion), channel_id=1, source_target_pairs={{0,16},{16,0},{32,48},{48,32},{64,80},{80,64},{96,112},{112,96},{1... | collective-permute-start | bytes 1179656 | tf_op jit(solution)/shard_map/ppermute | solution.py:270
  13.2 2.3 %collective-permute-start.4 = (bf16[256,512]{1,0:T(8,128)(2,1)S(1)}, bf16[256,512]{1,0:T(8,128)(2,1)S(1)}, u32[]{:S(2)}, u32[]{:S(2)}) collective-permute-start(bf16[256,512]{1,0:T(8,128)(2,1)S(1)} %pad_maximum_fusion.1), channel_id=1, source_target_pairs={{0,128},{16,144},{32,160},{48,176},{64,192},{80,208},{96,224},{112... | collective-permute-start | bytes 786440 | tf_op jit(solution)/shard_map/ppermute | solution.py:270
  15.5 1.7 %collective-permute-start.6 = (bf16[128,512]{1,0:T(8,128)(2,1)S(1)}, bf16[128,512]{1,0:T(8,128)(2,1)S(1)}, u32[]{:S(2)}, u32[]{:S(2)}) collective-permute-start(bf16[128,512]{1,0:T(8,128)(2,1)S(1)} %collective-permute-done.refs_4_), channel_id=1, source_target_pairs={{0,64},{16,80},{32,96},{48,112},{64,0},{80,16},{96,32},{112,48},{1... | collective-permute-start | bytes 393224 | tf_op jit(solution)/shard_map/ppermute | solution.py:270
  17.2 1.5 %collective-permute-start.5 = (bf16[128,512]{1,0:T(8,128)(2,1)S(1)}, bf16[128,512]{1,0:T(8,128)(2,1)S(1)}, u32[]{:S(2)}, u32[]{:S(2)}) collective-permute-start(bf16[128,512]{1,0:T(8,128)(2,1)S(1)} %collective-permute-done.1.refs_6_), channel_id=1, source_target_pairs={{0,32},{16,48},{32,64},{48,80},{64,96},{80,112},{96,0},{112,16},{1... | collective-permute-start | bytes 393224 | tf_op jit(solution)/shard_map/ppermute | solution.py:281
  19.4 2.2 %copy-done = bf16[128,128,128]{2,1,0:T(8,128)(2,1)S(1)} copy-done((bf16[128,128,128]{2,1,0:T(8,128)(2,1)S(1)}, bf16[128,128,128]{2,1,0:T(8,128)(2,1)}, u32[]{:S(2)}) %copy-start) | copy-done | bytes 4194328
  21.6 3.5 %dense_build.1.refs_0_ = bf16[2048,2048]{1,0:T(8,128)(2,1)S(1)} custom-call(s32[1]{0:T(128)S(6)} %copy.12.counts_ref, s32[256]{0:T(256)S(1)} %reshape.23.places_ref, bf16[128,128,128]{2,1,0:T(8,128)(2,1)S(1)} %copy-done), custom_call_target="tpu_custom_call" | custom-call | bytes 12582912 | tf_op jit(solution)/shard_map/dense_build/pallas_call | solution.py:70
  25.2 0.9 collective-permute-start.8
  26.4 1.3 collective-permute-done.8.refs_1_
  27.7 0.7 rows_middle.1
  28.5 1.5 %collective-permute-start.9 = (bf16[128,512]{1,0:T(8,128)(2,1)S(1)}, bf16[128,512]{1,0:T(8,128)(2,1)S(1)}, u32[]{:S(2)}, u32[]{:S(2)}) collective-permute-start(bf16[128,512]{1,0:T(8,128)(2,1)S(1)} %get-tuple-element.86), channel_id=1, source_target_pairs={{0,2},{2,4},{4,6},{6,8},{8,10},{10,12},{12,14},{14,0},{1,3},{3,5},... | collective-permute-start | bytes 393224 | tf_op jit(solution)/shard_map/ppermute | solution.py:285
  30.0 4.2 %collective-permute-start.10 = (bf16[128,512]{1,0:T(8,128)(2,1)S(1)}, bf16[128,512]{1,0:T(8,128)(2,1)S(1)}, u32[]{:S(2)}, u32[]{:S(2)}) collective-permute-start(bf16[128,512]{1,0:T(8,128)(2,1)S(1)} %get-tuple-element.87), channel_id=1, source_target_pairs={{0,14},{2,0},{4,2},{6,4},{8,6},{10,8},{12,10},{14,12},{1,15},{3,1}... | collective-permute-start | bytes 393224 | tf_op jit(solution)/shard_map/ppermute | solution.py:285
  34.2 1.5 %rows_outer.1 = bf16[512,512]{1,0:T(8,128)(2,1)S(1)} custom-call(bf16[2048,2048]{1,0:T(8,128)(2,1)S(1)} %dense_build.1.refs_0_, bf16[512,512]{1,0:T(8,128)(2,1)S(1)} %collective-permute-done.8.refs_1_, bf16[512,512]{1,0:T(8,128)(2,1)S(1)} %constant_dynamic-update-slice_fusion.refs_2_, bf16[384,512]{1,0:T(8,128)(2,1)S(1)} %collective-permute-done.7.refs_3_, ...), custom_call_target="tpu_custom_call" | custom-call | flops 1073741824 | bytes 2097152 | tf_op jit(solution)/shard_map/rows_outer/pallas_call | solution.py:104
  35.8 1.9 %collective-permute-done.9 = bf16[128,512]{1,0:T(8,128)(2,1)S(1)} collective-permute-done((bf16[128,512]{1,0:T(8,128)(2,1)S(1)}, bf16[128,512]{1,0:T(8,128)(2,1)S(1)}, u32[]{:S(2)}, u32[]{:S(2)}) %collective-permute-start.9) | collective-permute-done | bytes 131104 | tf_op jit(solution)/shard_map/ppermute | solution.py:285
  37.9 2.7 %collective-permute-start.13 = (bf16[256,512]{1,0:T(8,128)(2,1)S(1)}, bf16[256,512]{1,0:T(8,128)(2,1)S(1)}, u32[]{:S(2)}, u32[]{:S(2)}) collective-permute-start(bf16[256,512]{1,0:T(8,128)(2,1)S(1)} %get-tuple-element.90), channel_id=1, source_target_pairs={{0,14},{2,0},{4,2},{6,4},{8,6},{10,8},{12,10},{14,12},{1,15},{3,1}... | collective-permute-start | bytes 786440 | tf_op jit(solution)/shard_map/ppermute | solution.py:285
  40.6 3.7 %rows_inner.1 = bf16[1280,512]{1,0:T(8,128)(2,1)S(1)} custom-call(bf16[2048,2048]{1,0:T(8,128)(2,1)S(1)} %dense_build.1.refs_0_, bf16[512,512]{1,0:T(8,128)(2,1)S(1)} %collective-permute-done.8.refs_1_, bf16[512,512]{1,0:T(8,128)(2,1)S(1)} %constant_dynamic-update-slice_fusion.refs_2_, bf16[384,512]{1,0:T(8,128)(2,1)S(1)} %collective-permute-done.7.refs_3_, ...), custom_call_target="tpu_custom_call" | custom-call | flops 2684354560 | bytes 5242880 | tf_op jit(solution)/shard_map/rows_inner/pallas_call | solution.py:104
  44.2 1.8 %collective-permute-done.12 = bf16[256,512]{1,0:T(8,128)(2,1)S(1)} collective-permute-done((bf16[256,512]{1,0:T(8,128)(2,1)S(1)}, bf16[256,512]{1,0:T(8,128)(2,1)S(1)}, u32[]{:S(2)}, u32[]{:S(2)}) %collective-permute-start.12) | collective-permute-done | bytes 262176 | tf_op jit(solution)/shard_map/ppermute | solution.py:285
  46.2 1.3 collective-permute-start.14
  47.5 1.6 %collective-permute-start.15 = (bf16[256,512]{1,0:T(8,128)(2,1)S(1)}, bf16[256,512]{1,0:T(8,128)(2,1)S(1)}, u32[]{:S(2)}, u32[]{:S(2)}) collective-permute-start(bf16[256,512]{1,0:T(8,128)(2,1)S(1)} %get-tuple-element.94), channel_id=1, source_target_pairs={{0,14},{2,0},{4,2},{6,4},{8,6},{10,8},{12,10},{14,12},{1,15},{3,1}... | collective-permute-start | bytes 786440 | tf_op jit(solution)/shard_map/ppermute | solution.py:285
  49.1 4.5 %collective-permute-done.14 = bf16[256,512]{1,0:T(8,128)(2,1)S(1)} collective-permute-done((bf16[256,512]{1,0:T(8,128)(2,1)S(1)}, bf16[256,512]{1,0:T(8,128)(2,1)S(1)}, u32[]{:S(2)}, u32[]{:S(2)}) %collective-permute-start.14) | collective-permute-done | bytes 262176 | tf_op jit(solution)/shard_map/ppermute | solution.py:285
  53.8 1.0 collective-permute-start.16
  54.8 1.8 %collective-permute-start.17 = (bf16[256,512]{1,0:T(8,128)(2,1)S(1)}, bf16[256,512]{1,0:T(8,128)(2,1)S(1)}, u32[]{:S(2)}, u32[]{:S(2)}) collective-permute-start(bf16[256,512]{1,0:T(8,128)(2,1)S(1)} %get-tuple-element.98), channel_id=1, source_target_pairs={{0,14},{2,0},{4,2},{6,4},{8,6},{10,8},{12,10},{14,12},{1,15},{3,1}... | collective-permute-start | bytes 786440 | tf_op jit(solution)/shard_map/ppermute | solution.py:285
  56.6 3.8 %collective-permute-done.16 = bf16[256,512]{1,0:T(8,128)(2,1)S(1)} collective-permute-done((bf16[256,512]{1,0:T(8,128)(2,1)S(1)}, bf16[256,512]{1,0:T(8,128)(2,1)S(1)}, u32[]{:S(2)}, u32[]{:S(2)}) %collective-permute-start.16) | collective-permute-done | bytes 262176 | tf_op jit(solution)/shard_map/ppermute | solution.py:285
  61.0 4.8 %collective-permute-done.18.theirs_ref = bf16[256,512]{1,0:T(8,128)(2,1)S(1)} collective-permute-done((bf16[256,512]{1,0:T(8,128)(2,1)S(1)}, bf16[256,512]{1,0:T(8,128)(2,1)S(1)}, u32[]{:S(2)}, u32[]{:S(2)}) %collective-permute-start.18) | collective-permute-done | bytes 262176 | tf_op jit(solution)/shard_map/ppermute | solution.py:293
  65.7 1.0 layer.1
  66.7 1.5 collective-permute-start.20
  68.2 1.2 collective-permute-start.19
  69.4 0.8 weight_part.1
  70.2 6.4 %collective-permute-start.21 = (bf16[128,512]{1,0:T(8,128)(2,1)S(1)}, bf16[128,512]{1,0:T(8,128)(2,1)S(1)}, u32[]{:S(2)}, u32[]{:S(2)}) collective-permute-start(bf16[128,512]{1,0:T(8,128)(2,1)S(1)} %get-tuple-element.108), channel_id=1, source_target_pairs={{0,16},{16,0},{32,48},{48,32},{64,80},{80,64},{96,112},{112,96},{1... | collective-permute-start | bytes 393224 | tf_op jit(solution)/shard_map/ppermute | solution.py:270
  76.6 1.0 collective-permute-done.21
  77.6 1.3 collective-permute-start.22
  79.2 0.8 collective-permute-start.26
  80.0 0.8 collective-permute-start.25
  80.7 1.7 %collective-permute-start.24 = (bf16[128,512]{1,0:T(8,128)(2,1)S(1)}, bf16[128,512]{1,0:T(8,128)(2,1)S(1)}, u32[]{:S(2)}, u32[]{:S(2)}) collective-permute-start(bf16[128,512]{1,0:T(8,128)(2,1)S(1)} %add_convert_fusion.12), channel_id=1, source_target_pairs={{0,32},{16,48},{32,0},{48,16},{64,96},{80,112},{96,64},{112,80},{1... | collective-permute-start | bytes 393224 | tf_op jit(solution)/shard_map/ppermute | solution.py:270
  82.4 3.2 %collective-permute-done.26 = bf16[128,512]{1,0:T(8,128)(2,1)S(1)} collective-permute-done((bf16[128,512]{1,0:T(8,128)(2,1)S(1)}, bf16[128,512]{1,0:T(8,128)(2,1)S(1)}, u32[]{:S(2)}, u32[]{:S(2)}) %collective-permute-start.26) | collective-permute-done | bytes 131104 | tf_op jit(solution)/shard_map/ppermute | solution.py:270
  85.6 0.9 collective-permute-done.24
  86.6 2.5 %collective-permute-start.27 = (bf16[512,256]{1,0:T(8,128)(2,1)S(1)}, bf16[512,256]{1,0:T(8,128)(2,1)S(1)}, u32[]{:S(2)}, u32[]{:S(2)}) collective-permute-start(bf16[512,256]{1,0:T(8,128)(2,1)S(1)} %collective-permute-done.22.refs_3_), channel_id=1, source_target_pairs={{0,14},{2,0},{4,2},{6,4},{8,6},{10,8},{12,10},{14,12},{1,15},{3,1}... | collective-permute-start | bytes 786440 | tf_op jit(solution)/shard_map/ppermute | solution.py:285
  89.4 5.0 %collective-permute-done.29 = bf16[128,512]{1,0:T(8,128)(2,1)S(1)} collective-permute-done((bf16[128,512]{1,0:T(8,128)(2,1)S(1)}, bf16[128,512]{1,0:T(8,128)(2,1)S(1)}, u32[]{:S(2)}, u32[]{:S(2)}) %collective-permute-start.29) | collective-permute-done | bytes 131104 | tf_op jit(solution)/shard_map/ppermute | solution.py:270
  94.4 1.1 collective-permute-done.28.refs_7_
  95.7 2.7 %collective-permute-start.31 = (bf16[256,256]{1,0:T(8,128)(2,1)S(1)}, bf16[256,256]{1,0:T(8,128)(2,1)S(1)}, u32[]{:S(2)}, u32[]{:S(2)}) collective-permute-start(bf16[256,256]{1,0:T(8,128)(2,1)S(1)} %slice.110), channel_id=1, source_target_pairs={{0,14},{2,0},{4,2},{6,4},{8,6},{10,8},{12,10},{14,12},{1,15},{3,1}... | collective-permute-start | bytes 393224 | tf_op jit(solution)/shard_map/ppermute | solution.py:285
  98.3 4.0 %collective-permute-done.30.refs_5_ = bf16[256,256]{1,0:T(8,128)(2,1)S(1)} collective-permute-done((bf16[256,256]{1,0:T(8,128)(2,1)S(1)}, bf16[256,256]{1,0:T(8,128)(2,1)S(1)}, u32[]{:S(2)}, u32[]{:S(2)}) %collective-permute-start.30) | collective-permute-done | bytes 131104 | tf_op jit(solution)/shard_map/ppermute | solution.py:285
  102.4 1.2 columns_other.1
  103.7 10.2 %collective-permute-start.33 = (bf16[4,512,128]{2,1,0:T(8,128)(2,1)S(1)}, bf16[4,512,128]{2,1,0:T(8,128)(2,1)S(1)}, u32[]{:S(2)}, u32[]{:S(2)}) collective-permute-start(bf16[4,512,128]{2,1,0:T(8,128)(2,1)S(1)} %columns_other.1), channel_id=1, source_target_pairs={{0,16},{16,0},{32,48},{48,32},{64,80},{80,64},{96,112},{112,96},{1... | collective-permute-start | bytes 1572872 | tf_op jit(solution)/shard_map/ppermute | solution.py:270
  114.1 4.1 %columns_rest.1 = bf16[12,512,128]{2,1,0:T(8,128)(2,1)S(1)} custom-call(bf16[2048,2048]{1,0:T(8,128)(2,1)S(1)} %dense_build.1.refs_0_, bf16[512,256]{1,0:T(8,128)(2,1)S(1)} %get-tuple-element.104.refs_1_, bf16[512,256]{1,0:T(8,128)(2,1)S(1)} %collective-permute-done.19.refs_2_, bf16[512,256]{1,0:T(8,128)(2,1)S(1)} %collective-permute-done.22.refs_3_, ...), custom_call_target="tpu_custom_call" | custom-call | flops 3221225472 | bytes 6291456 | tf_op jit(solution)/shard_map/columns_rest/pallas_call | solution.py:144
  118.2 4.4 %collective-permute-done.34 = bf16[128,512]{1,0:T(8,128)(2,1)S(1)} collective-permute-done((bf16[128,512]{1,0:T(8,128)(2,1)S(1)}, bf16[128,512]{1,0:T(8,128)(2,1)S(1)}, u32[]{:S(2)}, u32[]{:S(2)}) %collective-permute-start.34) | collective-permute-done | bytes 131104 | tf_op jit(solution)/shard_map/ppermute | solution.py:289
  123.3 0.7 collective-permute-start.38
  124.0 3.1 %collective-permute-start.39 = (bf16[128,512]{1,0:T(8,128)(2,1)S(1)}, bf16[128,512]{1,0:T(8,128)(2,1)S(1)}, u32[]{:S(2)}, u32[]{:S(2)}) collective-permute-start(bf16[128,512]{1,0:T(8,128)(2,1)S(1)} %add_convert_fusion.8), channel_id=1, source_target_pairs={{0,8},{2,10},{4,12},{6,14},{8,0},{10,2},{12,4},{14,6},{1,9},{3,11}... | collective-permute-start | bytes 393224 | tf_op jit(solution)/shard_map/ppermute | solution.py:289
  127.1 1.7 %collective-permute-start.37 = (bf16[512,128]{1,0:T(8,128)(2,1)S(1)}, bf16[512,128]{1,0:T(8,128)(2,1)S(1)}, u32[]{:S(2)}, u32[]{:S(2)}) collective-permute-start(bf16[512,128]{1,0:T(8,128)(2,1)S(1)} %get-tuple-element.157), channel_id=1, source_target_pairs={{0,96},{16,112},{32,0},{48,16},{64,32},{80,48},{96,64},{112,80},{1... | collective-permute-start | bytes 393224 | tf_op jit(solution)/shard_map/ppermute | solution.py:281
  128.9 7.4 %collective-permute-done.39 = bf16[128,512]{1,0:T(8,128)(2,1)S(1)} collective-permute-done((bf16[128,512]{1,0:T(8,128)(2,1)S(1)}, bf16[128,512]{1,0:T(8,128)(2,1)S(1)}, u32[]{:S(2)}, u32[]{:S(2)}) %collective-permute-start.39) | collective-permute-done | bytes 131104 | tf_op jit(solution)/shard_map/ppermute | solution.py:289
  136.5 1.2 collective-permute-start.46
  137.7 0.7 collective-permute-start.45
  138.7 2.5 %collective-permute-start.40 = (bf16[512,128]{1,0:T(8,128)(2,1)S(1)}, bf16[512,128]{1,0:T(8,128)(2,1)S(1)}, u32[]{:S(2)}, u32[]{:S(2)}) collective-permute-start(bf16[512,128]{1,0:T(8,128)(2,1)S(1)} %get-tuple-element.144), channel_id=1, source_target_pairs={{0,128},{16,144},{32,160},{48,176},{64,192},{80,208},{96,224},{112... | collective-permute-start | bytes 393224 | tf_op jit(solution)/shard_map/ppermute | solution.py:270
  141.4 1.0 collective-permute-done.46.refs_4_
  142.4 1.9 %collective-permute-start.42 = (bf16[512,128]{1,0:T(8,128)(2,1)S(1)}, bf16[512,128]{1,0:T(8,128)(2,1)S(1)}, u32[]{:S(2)}, u32[]{:S(2)}) collective-permute-start(bf16[512,128]{1,0:T(8,128)(2,1)S(1)} %get-tuple-element.146), channel_id=1, source_target_pairs={{0,96},{16,112},{32,0},{48,16},{64,32},{80,48},{96,64},{112,80},{1... | collective-permute-start | bytes 393224 | tf_op jit(solution)/shard_map/ppermute | solution.py:281
  144.3 0.7 collective-permute-done.45.refs_3_
  145.0 0.9 collective-permute-start.43
  145.9 1.6 %weight_place.1 = f32[512,512]{1,0:T(8,128)} custom-call(s32[2]{0:T(128)S(1)} %pad_add_fusion.1.where_ref.refs_0_, bf16[128,512]{1,0:T(8,128)(2,1)S(1)} %add_convert_fusion.6.refs_1_, bf16[128,512]{1,0:T(8,128)(2,1)S(1)} %collective-permute-done.44.refs_2_, bf16[128,512]{1,0:T(8,128)(2,1)S(1)} %collective-permute-done.45.refs_3_, ...), custom_call_target="tpu_custom_call" | custom-call | tf_op jit(solution)/shard_map/weight_place/pallas_call | solution.py:259
  147.5 1.9 %collective-permute-done.40.refs_1_ = bf16[512,128]{1,0:T(8,128)(2,1)S(1)} collective-permute-done((bf16[512,128]{1,0:T(8,128)(2,1)S(1)}, bf16[512,128]{1,0:T(8,128)(2,1)S(1)}, u32[]{:S(2)}, u32[]{:S(2)}) %collective-permute-start.40) | collective-permute-done | bytes 131104 | tf_op jit(solution)/shard_map/ppermute | solution.py:270
  149.4 0.8 finish.1
  (80 shorter events, 5.7 us)
Async XLA Ops:
  0.6 8.1 %collective-permute-start.3 = (bf16[128,512]{1,0:T(8,128)(2,1)}, bf16[128,512]{1,0:T(8,128)(2,1)S(1)}, u32[]{:S(2)}, u32[]{:S(2)}) collective-permute-start(bf16[128,512]{1,0:T(8,128)(2,1)} %refs_8_.5), channel_id=1, source_target_pairs={{0,16},{16,0},{32,48},{48,32},{64,80},{80,64},{96,112},{112,96},{1... | collective-permute-start | bytes 393224 | tf_op jit(solution)/shard_map/ppermute | solution.py:270
  4.0 5.3 %collective-permute-start.2 = (bf16[128,512]{1,0:T(8,128)(2,1)}, bf16[128,512]{1,0:T(8,128)(2,1)S(1)}, u32[]{:S(2)}, u32[]{:S(2)}) collective-permute-start(bf16[128,512]{1,0:T(8,128)(2,1)} %refs_8_.5), channel_id=1, source_target_pairs={{0,96},{16,112},{32,0},{48,16},{64,32},{80,48},{96,64},{112,80},{1... | collective-permute-start | bytes 393224 | tf_op jit(solution)/shard_map/ppermute | solution.py:281
  4.7 6.1 %collective-permute-start.1 = (bf16[128,512]{1,0:T(8,128)(2,1)}, bf16[128,512]{1,0:T(8,128)(2,1)S(1)}, u32[]{:S(2)}, u32[]{:S(2)}) collective-permute-start(bf16[128,512]{1,0:T(8,128)(2,1)} %refs_8_.5), channel_id=1, source_target_pairs={{0,32},{16,48},{32,64},{48,80},{64,96},{80,112},{96,0},{112,16},{1... | collective-permute-start | bytes 393224 | tf_op jit(solution)/shard_map/ppermute | solution.py:281
  5.4 6.1 %collective-permute-start = (bf16[128,512]{1,0:T(8,128)(2,1)}, bf16[128,512]{1,0:T(8,128)(2,1)S(1)}, u32[]{:S(2)}, u32[]{:S(2)}) collective-permute-start(bf16[128,512]{1,0:T(8,128)(2,1)} %refs_8_.5), channel_id=1, source_target_pairs={{0,128},{16,144},{32,160},{48,176},{64,192},{80,208},{96,224},{112... | collective-permute-start | bytes 393224 | tf_op jit(solution)/shard_map/ppermute | solution.py:270
  11.6 13.6 %collective-permute-start.7 = (bf16[384,512]{1,0:T(8,128)(2,1)S(1)}, bf16[384,512]{1,0:T(8,128)(2,1)S(1)}, u32[]{:S(2)}, u32[]{:S(2)}) collective-permute-start(bf16[384,512]{1,0:T(8,128)(2,1)S(1)} %pad_maximum_fusion), channel_id=1, source_target_pairs={{0,16},{16,0},{32,48},{48,32},{64,80},{80,64},{96,112},{112,96},{1... | collective-permute-start | bytes 1179656 | tf_op jit(solution)/shard_map/ppermute | solution.py:270
  13.2 12.0 %collective-permute-start.4 = (bf16[256,512]{1,0:T(8,128)(2,1)S(1)}, bf16[256,512]{1,0:T(8,128)(2,1)S(1)}, u32[]{:S(2)}, u32[]{:S(2)}) collective-permute-start(bf16[256,512]{1,0:T(8,128)(2,1)S(1)} %pad_maximum_fusion.1), channel_id=1, source_target_pairs={{0,128},{16,144},{32,160},{48,176},{64,192},{80,208},{96,224},{112... | collective-permute-start | bytes 786440 | tf_op jit(solution)/shard_map/ppermute | solution.py:270
  15.5 9.7 %collective-permute-start.6 = (bf16[128,512]{1,0:T(8,128)(2,1)S(1)}, bf16[128,512]{1,0:T(8,128)(2,1)S(1)}, u32[]{:S(2)}, u32[]{:S(2)}) collective-permute-start(bf16[128,512]{1,0:T(8,128)(2,1)S(1)} %collective-permute-done.refs_4_), channel_id=1, source_target_pairs={{0,64},{16,80},{32,96},{48,112},{64,0},{80,16},{96,32},{112,48},{1... | collective-permute-start | bytes 393224 | tf_op jit(solution)/shard_map/ppermute | solution.py:270
  17.2 7.9 %collective-permute-start.5 = (bf16[128,512]{1,0:T(8,128)(2,1)S(1)}, bf16[128,512]{1,0:T(8,128)(2,1)S(1)}, u32[]{:S(2)}, u32[]{:S(2)}) collective-permute-start(bf16[128,512]{1,0:T(8,128)(2,1)S(1)} %collective-permute-done.1.refs_6_), channel_id=1, source_target_pairs={{0,32},{16,48},{32,64},{48,80},{64,96},{80,112},{96,0},{112,16},{1... | collective-permute-start | bytes 393224 | tf_op jit(solution)/shard_map/ppermute | solution.py:281
  19.4 2.2 %copy-start = (bf16[128,128,128]{2,1,0:T(8,128)(2,1)S(1)}, bf16[128,128,128]{2,1,0:T(8,128)(2,1)}, u32[]{:S(2)}) copy-start(bf16[128,128,128]{2,1,0:T(8,128)(2,1)} %tiles_ref.1) | copy-start | bytes 12582916
  21.6 4.6 %copy-start.3 = (bf16[128,512]{1,0:T(8,128)(2,1)S(1)}, bf16[128,512]{1,0:T(8,128)(2,1)}, u32[]{:S(2)}) copy-start(bf16[128,512]{1,0:T(8,128)(2,1)} %cot_ref.1) | copy-start | bytes 393220
  21.6 6.1 %copy-start.1 = (bf16[128,512]{1,0:T(8,128)(2,1)S(1)}, bf16[128,512]{1,0:T(8,128)(2,1)}, u32[]{:S(2)}) copy-start(bf16[128,512]{1,0:T(8,128)(2,1)} %refs_8_.5) | copy-start | bytes 393220
  25.2 2.5 %collective-permute-start.8 = (bf16[512,512]{1,0:T(8,128)(2,1)S(1)}, bf16[512,512]{1,0:T(8,128)(2,1)S(1)}, u32[]{:S(2)}, u32[]{:S(2)}) collective-permute-start(bf16[512,512]{1,0:T(8,128)(2,1)S(1)} %constant_dynamic-update-slice_fusion.refs_2_), channel_id=1, source_target_pairs={{0,16},{16,0},{32,48},{48,32},{64,80},{80,64},{96,112},{112,96},{1... | collective-permute-start | bytes 1572872 | tf_op jit(solution)/shard_map/ppermute | solution.py:270
  26.2 11.6 %collective-permute-start.11 = (bf16[128,512]{1,0:T(8,128)(2,1)S(1)}, bf16[128,512]{1,0:T(8,128)(2,1)S(1)}, u32[]{:S(2)}, u32[]{:S(2)}) collective-permute-start(bf16[128,512]{1,0:T(8,128)(2,1)S(1)} %copy-done.3), channel_id=1, source_target_pairs={{0,1},{1,0},{2,3},{3,2},{4,5},{5,4},{6,7},{7,6},{8,9},{9,8},{10,11... | collective-permute-start | bytes 393224 | tf_op jit(solution)/shard_map/ppermute | solution.py:293
  28.5 9.2 %collective-permute-start.9 = (bf16[128,512]{1,0:T(8,128)(2,1)S(1)}, bf16[128,512]{1,0:T(8,128)(2,1)S(1)}, u32[]{:S(2)}, u32[]{:S(2)}) collective-permute-start(bf16[128,512]{1,0:T(8,128)(2,1)S(1)} %get-tuple-element.86), channel_id=1, source_target_pairs={{0,2},{2,4},{4,6},{6,8},{8,10},{10,12},{12,14},{14,0},{1,3},{3,5},... | collective-permute-start | bytes 393224 | tf_op jit(solution)/shard_map/ppermute | solution.py:285
  30.0 7.7 %collective-permute-start.10 = (bf16[128,512]{1,0:T(8,128)(2,1)S(1)}, bf16[128,512]{1,0:T(8,128)(2,1)S(1)}, u32[]{:S(2)}, u32[]{:S(2)}) collective-permute-start(bf16[128,512]{1,0:T(8,128)(2,1)S(1)} %get-tuple-element.87), channel_id=1, source_target_pairs={{0,14},{2,0},{4,2},{6,4},{8,6},{10,8},{12,10},{14,12},{1,15},{3,1}... | collective-permute-start | bytes 393224 | tf_op jit(solution)/shard_map/ppermute | solution.py:285
  37.8 8.2 %collective-permute-start.12 = (bf16[256,512]{1,0:T(8,128)(2,1)S(1)}, bf16[256,512]{1,0:T(8,128)(2,1)S(1)}, u32[]{:S(2)}, u32[]{:S(2)}) collective-permute-start(bf16[256,512]{1,0:T(8,128)(2,1)S(1)} %get-tuple-element.89), channel_id=1, source_target_pairs={{0,2},{2,4},{4,6},{6,8},{8,10},{10,12},{12,14},{14,0},{1,3},{3,5},... | collective-permute-start | bytes 786440 | tf_op jit(solution)/shard_map/ppermute | solution.py:285
  37.9 8.1 %collective-permute-start.13 = (bf16[256,512]{1,0:T(8,128)(2,1)S(1)}, bf16[256,512]{1,0:T(8,128)(2,1)S(1)}, u32[]{:S(2)}, u32[]{:S(2)}) collective-permute-start(bf16[256,512]{1,0:T(8,128)(2,1)S(1)} %get-tuple-element.90), channel_id=1, source_target_pairs={{0,14},{2,0},{4,2},{6,4},{8,6},{10,8},{12,10},{14,12},{1,15},{3,1}... | collective-permute-start | bytes 786440 | tf_op jit(solution)/shard_map/ppermute | solution.py:285
  46.2 19.6 %copy-start.2 = (bf16[512,512]{1,0:T(8,128)(2,1)S(1)}, bf16[512,512]{1,0:T(8,128)(2,1)}, u32[]{:S(2)}) copy-start(bf16[512,512]{1,0:T(8,128)(2,1)} %weight_ref.1) | copy-start | bytes 1572868
  46.2 7.5 %collective-permute-start.14 = (bf16[256,512]{1,0:T(8,128)(2,1)S(1)}, bf16[256,512]{1,0:T(8,128)(2,1)S(1)}, u32[]{:S(2)}, u32[]{:S(2)}) collective-permute-start(bf16[256,512]{1,0:T(8,128)(2,1)S(1)} %get-tuple-element.93), channel_id=1, source_target_pairs={{0,2},{2,4},{4,6},{6,8},{8,10},{10,12},{12,14},{14,0},{1,3},{3,5},... | collective-permute-start | bytes 786440 | tf_op jit(solution)/shard_map/ppermute | solution.py:285
  47.5 6.2 %collective-permute-start.15 = (bf16[256,512]{1,0:T(8,128)(2,1)S(1)}, bf16[256,512]{1,0:T(8,128)(2,1)S(1)}, u32[]{:S(2)}, u32[]{:S(2)}) collective-permute-start(bf16[256,512]{1,0:T(8,128)(2,1)S(1)} %get-tuple-element.94), channel_id=1, source_target_pairs={{0,14},{2,0},{4,2},{6,4},{8,6},{10,8},{12,10},{14,12},{1,15},{3,1}... | collective-permute-start | bytes 786440 | tf_op jit(solution)/shard_map/ppermute | solution.py:285
  53.8 6.5 %collective-permute-start.16 = (bf16[256,512]{1,0:T(8,128)(2,1)S(1)}, bf16[256,512]{1,0:T(8,128)(2,1)S(1)}, u32[]{:S(2)}, u32[]{:S(2)}) collective-permute-start(bf16[256,512]{1,0:T(8,128)(2,1)S(1)} %get-tuple-element.97), channel_id=1, source_target_pairs={{0,2},{2,4},{4,6},{6,8},{8,10},{10,12},{12,14},{14,0},{1,3},{3,5},... | collective-permute-start | bytes 786440 | tf_op jit(solution)/shard_map/ppermute | solution.py:285
  54.8 5.5 %collective-permute-start.17 = (bf16[256,512]{1,0:T(8,128)(2,1)S(1)}, bf16[256,512]{1,0:T(8,128)(2,1)S(1)}, u32[]{:S(2)}, u32[]{:S(2)}) collective-permute-start(bf16[256,512]{1,0:T(8,128)(2,1)S(1)} %get-tuple-element.98), channel_id=1, source_target_pairs={{0,14},{2,0},{4,2},{6,4},{8,6},{10,8},{12,10},{14,12},{1,15},{3,1}... | collective-permute-start | bytes 786440 | tf_op jit(solution)/shard_map/ppermute | solution.py:285
  60.4 5.3 %collective-permute-start.18 = (bf16[256,512]{1,0:T(8,128)(2,1)S(1)}, bf16[256,512]{1,0:T(8,128)(2,1)S(1)}, u32[]{:S(2)}, u32[]{:S(2)}) collective-permute-start(bf16[256,512]{1,0:T(8,128)(2,1)S(1)} %add_convert_fusion.1.mine_ref), channel_id=1, source_target_pairs={{0,1},{1,0},{2,3},{3,2},{4,5},{5,4},{6,7},{7,6},{8,9},{9,8},{10,11... | collective-permute-start | bytes 786440 | tf_op jit(solution)/shard_map/ppermute | solution.py:293
  66.7 10.9 %collective-permute-start.20 = (bf16[512,256]{1,0:T(8,128)(2,1)S(1)}, bf16[512,256]{1,0:T(8,128)(2,1)S(1)}, u32[]{:S(2)}, u32[]{:S(2)}) collective-permute-start(bf16[512,256]{1,0:T(8,128)(2,1)S(1)} %get-tuple-element.104.refs_1_), channel_id=1, source_target_pairs={{0,2},{2,4},{4,6},{6,8},{8,10},{10,12},{12,14},{14,0},{1,3},{3,5},... | collective-permute-start | bytes 786440 | tf_op jit(solution)/shard_map/ppermute | solution.py:285
  68.2 9.4 %collective-permute-start.19 = (bf16[512,256]{1,0:T(8,128)(2,1)S(1)}, bf16[512,256]{1,0:T(8,128)(2,1)S(1)}, u32[]{:S(2)}, u32[]{:S(2)}) collective-permute-start(bf16[512,256]{1,0:T(8,128)(2,1)S(1)} %get-tuple-element.104.refs_1_), channel_id=1, source_target_pairs={{0,14},{2,0},{4,2},{6,4},{8,6},{10,8},{12,10},{14,12},{1,15},{3,1}... | collective-permute-start | bytes 786440 | tf_op jit(solution)/shard_map/ppermute | solution.py:285
  70.2 7.4 %collective-permute-start.21 = (bf16[128,512]{1,0:T(8,128)(2,1)S(1)}, bf16[128,512]{1,0:T(8,128)(2,1)S(1)}, u32[]{:S(2)}, u32[]{:S(2)}) collective-permute-start(bf16[128,512]{1,0:T(8,128)(2,1)S(1)} %get-tuple-element.108), channel_id=1, source_target_pairs={{0,16},{16,0},{32,48},{48,32},{64,80},{80,64},{96,112},{112,96},{1... | collective-permute-start | bytes 393224 | tf_op jit(solution)/shard_map/ppermute | solution.py:270
  77.6 8.9 %collective-permute-start.22 = (bf16[512,256]{1,0:T(8,128)(2,1)S(1)}, bf16[512,256]{1,0:T(8,128)(2,1)S(1)}, u32[]{:S(2)}, u32[]{:S(2)}) collective-permute-start(bf16[512,256]{1,0:T(8,128)(2,1)S(1)} %collective-permute-done.19.refs_2_), channel_id=1, source_target_pairs={{0,14},{2,0},{4,2},{6,4},{8,6},{10,8},{12,10},{14,12},{1,15},{3,1}... | collective-permute-start | bytes 786440 | tf_op jit(solution)/shard_map/ppermute | solution.py:285
  78.9 7.6 %collective-permute-start.23 = (bf16[512,256]{1,0:T(8,128)(2,1)S(1)}, bf16[512,256]{1,0:T(8,128)(2,1)S(1)}, u32[]{:S(2)}, u32[]{:S(2)}) collective-permute-start(bf16[512,256]{1,0:T(8,128)(2,1)S(1)} %collective-permute-done.20.refs_9_), channel_id=1, source_target_pairs={{0,2},{2,4},{4,6},{6,8},{8,10},{10,12},{12,14},{14,0},{1,3},{3,5},... | collective-permute-start | bytes 786440 | tf_op jit(solution)/shard_map/ppermute | solution.py:285
  79.2 6.4 %collective-permute-start.26 = (bf16[128,512]{1,0:T(8,128)(2,1)S(1)}, bf16[128,512]{1,0:T(8,128)(2,1)S(1)}, u32[]{:S(2)}, u32[]{:S(2)}) collective-permute-start(bf16[128,512]{1,0:T(8,128)(2,1)S(1)} %add_convert_fusion.12), channel_id=1, source_target_pairs={{0,96},{16,112},{32,64},{48,80},{64,32},{80,48},{96,0},{112,16},{1... | collective-permute-start | bytes 393224 | tf_op jit(solution)/shard_map/ppermute | solution.py:270
  80.0 5.6 %collective-permute-start.25 = (bf16[128,512]{1,0:T(8,128)(2,1)S(1)}, bf16[128,512]{1,0:T(8,128)(2,1)S(1)}, u32[]{:S(2)}, u32[]{:S(2)}) collective-permute-start(bf16[128,512]{1,0:T(8,128)(2,1)S(1)} %add_convert_fusion.12), channel_id=1, source_target_pairs={{0,64},{16,80},{32,96},{48,112},{64,0},{80,16},{96,32},{112,48},{1... | collective-permute-start | bytes 393224 | tf_op jit(solution)/shard_map/ppermute | solution.py:270
  80.7 5.7 %collective-permute-start.24 = (bf16[128,512]{1,0:T(8,128)(2,1)S(1)}, bf16[128,512]{1,0:T(8,128)(2,1)S(1)}, u32[]{:S(2)}, u32[]{:S(2)}) collective-permute-start(bf16[128,512]{1,0:T(8,128)(2,1)S(1)} %add_convert_fusion.12), channel_id=1, source_target_pairs={{0,32},{16,48},{32,0},{48,16},{64,96},{80,112},{96,64},{112,80},{1... | collective-permute-start | bytes 393224 | tf_op jit(solution)/shard_map/ppermute | solution.py:270
  86.6 7.8 %collective-permute-start.27 = (bf16[512,256]{1,0:T(8,128)(2,1)S(1)}, bf16[512,256]{1,0:T(8,128)(2,1)S(1)}, u32[]{:S(2)}, u32[]{:S(2)}) collective-permute-start(bf16[512,256]{1,0:T(8,128)(2,1)S(1)} %collective-permute-done.22.refs_3_), channel_id=1, source_target_pairs={{0,14},{2,0},{4,2},{6,4},{8,6},{10,8},{12,10},{14,12},{1,15},{3,1}... | collective-permute-start | bytes 786440 | tf_op jit(solution)/shard_map/ppermute | solution.py:285
  89.1 6.4 %collective-permute-start.28 = (bf16[512,256]{1,0:T(8,128)(2,1)S(1)}, bf16[512,256]{1,0:T(8,128)(2,1)S(1)}, u32[]{:S(2)}, u32[]{:S(2)}) collective-permute-start(bf16[512,256]{1,0:T(8,128)(2,1)S(1)} %collective-permute-done.23.refs_8_), channel_id=1, source_target_pairs={{0,2},{2,4},{4,6},{6,8},{8,10},{10,12},{12,14},{14,0},{1,3},{3,5},... | collective-permute-start | bytes 786440 | tf_op jit(solution)/shard_map/ppermute | solution.py:285
  89.1 5.3 %collective-permute-start.29 = (bf16[128,512]{1,0:T(8,128)(2,1)S(1)}, bf16[128,512]{1,0:T(8,128)(2,1)S(1)}, u32[]{:S(2)}, u32[]{:S(2)}) collective-permute-start(bf16[128,512]{1,0:T(8,128)(2,1)S(1)} %add_convert_fusion.11), channel_id=1, source_target_pairs={{0,128},{16,144},{32,160},{48,176},{64,192},{80,208},{96,224},{112... | collective-permute-start | bytes 393224 | tf_op jit(solution)/shard_map/ppermute | solution.py:270
  95.6 6.7 %collective-permute-start.30 = (bf16[256,256]{1,0:T(8,128)(2,1)S(1)}, bf16[256,256]{1,0:T(8,128)(2,1)S(1)}, u32[]{:S(2)}, u32[]{:S(2)}) collective-permute-start(bf16[256,256]{1,0:T(8,128)(2,1)S(1)} %slice.109), channel_id=1, source_target_pairs={{0,2},{2,4},{4,6},{6,8},{8,10},{10,12},{12,14},{14,0},{1,3},{3,5},... | collective-permute-start | bytes 393224 | tf_op jit(solution)/shard_map/ppermute | solution.py:285
  95.7 6.7 %collective-permute-start.31 = (bf16[256,256]{1,0:T(8,128)(2,1)S(1)}, bf16[256,256]{1,0:T(8,128)(2,1)S(1)}, u32[]{:S(2)}, u32[]{:S(2)}) collective-permute-start(bf16[256,256]{1,0:T(8,128)(2,1)S(1)} %slice.110), channel_id=1, source_target_pairs={{0,14},{2,0},{4,2},{6,4},{8,6},{10,8},{12,10},{14,12},{1,15},{3,1}... | collective-permute-start | bytes 393224 | tf_op jit(solution)/shard_map/ppermute | solution.py:285
  98.3 4.1 %collective-permute-start.32 = (bf16[128,512]{1,0:T(8,128)(2,1)S(1)}, bf16[128,512]{1,0:T(8,128)(2,1)S(1)}, u32[]{:S(2)}, u32[]{:S(2)}) collective-permute-start(bf16[128,512]{1,0:T(8,128)(2,1)S(1)} %add_convert_fusion.10), channel_id=1, source_target_pairs={{0,2},{2,0},{4,6},{6,4},{8,10},{10,8},{12,14},{14,12},{1,3},{3,1},... | collective-permute-start | bytes 393224 | tf_op jit(solution)/shard_map/ppermute | solution.py:289
  103.7 18.9 %collective-permute-start.33 = (bf16[4,512,128]{2,1,0:T(8,128)(2,1)S(1)}, bf16[4,512,128]{2,1,0:T(8,128)(2,1)S(1)}, u32[]{:S(2)}, u32[]{:S(2)}) collective-permute-start(bf16[4,512,128]{2,1,0:T(8,128)(2,1)S(1)} %columns_other.1), channel_id=1, source_target_pairs={{0,16},{16,0},{32,48},{48,32},{64,80},{80,64},{96,112},{112,96},{1... | collective-permute-start | bytes 1572872 | tf_op jit(solution)/shard_map/ppermute | solution.py:270
  113.9 8.7 %collective-permute-start.34 = (bf16[128,512]{1,0:T(8,128)(2,1)S(1)}, bf16[128,512]{1,0:T(8,128)(2,1)S(1)}, u32[]{:S(2)}, u32[]{:S(2)}) collective-permute-start(bf16[128,512]{1,0:T(8,128)(2,1)S(1)} %add_convert_fusion.9), channel_id=1, source_target_pairs={{0,4},{2,6},{4,0},{6,2},{8,12},{10,14},{12,8},{14,10},{1,5},{3,7},... | collective-permute-start | bytes 393224 | tf_op jit(solution)/shard_map/ppermute | solution.py:289
  122.9 13.4 %collective-permute-start.35 = (bf16[2,512,128]{2,1,0:T(8,128)(2,1)S(1)}, bf16[2,512,128]{2,1,0:T(8,128)(2,1)S(1)}, u32[]{:S(2)}, u32[]{:S(2)}) collective-permute-start(bf16[2,512,128]{2,1,0:T(8,128)(2,1)S(1)} %slice.115), channel_id=1, source_target_pairs={{0,128},{16,144},{32,160},{48,176},{64,192},{80,208},{96,224},{112... | collective-permute-start | bytes 786440 | tf_op jit(solution)/shard_map/ppermute | solution.py:270
  123.3 13.0 %collective-permute-start.38 = (bf16[3,512,128]{2,1,0:T(8,128)(2,1)S(1)}, bf16[3,512,128]{2,1,0:T(8,128)(2,1)S(1)}, u32[]{:S(2)}, u32[]{:S(2)}) collective-permute-start(bf16[3,512,128]{2,1,0:T(8,128)(2,1)S(1)} %slice.114), channel_id=1, source_target_pairs={{0,16},{16,0},{32,48},{48,32},{64,80},{80,64},{96,112},{112,96},{1... | collective-permute-start | bytes 1179656 | tf_op jit(solution)/shard_map/ppermute | solution.py:270
  124.0 12.2 %collective-permute-start.39 = (bf16[128,512]{1,0:T(8,128)(2,1)S(1)}, bf16[128,512]{1,0:T(8,128)(2,1)S(1)}, u32[]{:S(2)}, u32[]{:S(2)}) collective-permute-start(bf16[128,512]{1,0:T(8,128)(2,1)S(1)} %add_convert_fusion.8), channel_id=1, source_target_pairs={{0,8},{2,10},{4,12},{6,14},{8,0},{10,2},{12,4},{14,6},{1,9},{3,11}... | collective-permute-start | bytes 393224 | tf_op jit(solution)/shard_map/ppermute | solution.py:289
  127.1 9.1 %collective-permute-start.37 = (bf16[512,128]{1,0:T(8,128)(2,1)S(1)}, bf16[512,128]{1,0:T(8,128)(2,1)S(1)}, u32[]{:S(2)}, u32[]{:S(2)}) collective-permute-start(bf16[512,128]{1,0:T(8,128)(2,1)S(1)} %get-tuple-element.157), channel_id=1, source_target_pairs={{0,96},{16,112},{32,0},{48,16},{64,32},{80,48},{96,64},{112,80},{1... | collective-permute-start | bytes 393224 | tf_op jit(solution)/shard_map/ppermute | solution.py:281
  128.8 7.4 %collective-permute-start.36 = (bf16[512,128]{1,0:T(8,128)(2,1)S(1)}, bf16[512,128]{1,0:T(8,128)(2,1)S(1)}, u32[]{:S(2)}, u32[]{:S(2)}) collective-permute-start(bf16[512,128]{1,0:T(8,128)(2,1)S(1)} %get-tuple-element.158), channel_id=1, source_target_pairs={{0,64},{16,80},{32,96},{48,112},{64,0},{80,16},{96,32},{112,48},{1... | collective-permute-start | bytes 393224 | tf_op jit(solution)/shard_map/ppermute | solution.py:270
  136.5 5.9 %collective-permute-start.46 = (bf16[128,512]{1,0:T(8,128)(2,1)S(1)}, bf16[128,512]{1,0:T(8,128)(2,1)S(1)}, u32[]{:S(2)}, u32[]{:S(2)}) collective-permute-start(bf16[128,512]{1,0:T(8,128)(2,1)S(1)} %add_convert_fusion.6.refs_1_), channel_id=1, source_target_pairs={{0,17},{1,16},{16,1},{17,0},{32,49},{33,48},{48,33},{49,32},{64,81... | collective-permute-start | bytes 393224 | tf_op jit(solution)/shard_map/ppermute | solution.py:298
  137.7 7.3 %collective-permute-start.45 = (bf16[128,512]{1,0:T(8,128)(2,1)S(1)}, bf16[128,512]{1,0:T(8,128)(2,1)S(1)}, u32[]{:S(2)}, u32[]{:S(2)}) collective-permute-start(bf16[128,512]{1,0:T(8,128)(2,1)S(1)} %add_convert_fusion.6.refs_1_), channel_id=1, source_target_pairs={{0,1},{1,0},{2,3},{3,2},{4,5},{5,4},{6,7},{7,6},{8,9},{9,8},{10,11... | collective-permute-start | bytes 393224 | tf_op jit(solution)/shard_map/ppermute | solution.py:293
  138.4 7.5 %collective-permute-start.44 = (bf16[128,512]{1,0:T(8,128)(2,1)S(1)}, bf16[128,512]{1,0:T(8,128)(2,1)S(1)}, u32[]{:S(2)}, u32[]{:S(2)}) collective-permute-start(bf16[128,512]{1,0:T(8,128)(2,1)S(1)} %add_convert_fusion.6.refs_1_), channel_id=1, source_target_pairs={{0,16},{16,0},{32,48},{48,32},{64,80},{80,64},{96,112},{112,96},{1... | collective-permute-start | bytes 393224 | tf_op jit(solution)/shard_map/ppermute | solution.py:270
  138.7 10.7 %collective-permute-start.40 = (bf16[512,128]{1,0:T(8,128)(2,1)S(1)}, bf16[512,128]{1,0:T(8,128)(2,1)S(1)}, u32[]{:S(2)}, u32[]{:S(2)}) collective-permute-start(bf16[512,128]{1,0:T(8,128)(2,1)S(1)} %get-tuple-element.144), channel_id=1, source_target_pairs={{0,128},{16,144},{32,160},{48,176},{64,192},{80,208},{96,224},{112... | collective-permute-start | bytes 393224 | tf_op jit(solution)/shard_map/ppermute | solution.py:270
  141.2 8.2 %collective-permute-start.41 = (bf16[512,128]{1,0:T(8,128)(2,1)S(1)}, bf16[512,128]{1,0:T(8,128)(2,1)S(1)}, u32[]{:S(2)}, u32[]{:S(2)}) collective-permute-start(bf16[512,128]{1,0:T(8,128)(2,1)S(1)} %fusion.2), channel_id=1, source_target_pairs={{0,32},{16,48},{32,64},{48,80},{64,96},{80,112},{96,0},{112,16},{1... | collective-permute-start | bytes 393224 | tf_op jit(solution)/shard_map/ppermute | solution.py:281
  142.4 7.0 %collective-permute-start.42 = (bf16[512,128]{1,0:T(8,128)(2,1)S(1)}, bf16[512,128]{1,0:T(8,128)(2,1)S(1)}, u32[]{:S(2)}, u32[]{:S(2)}) collective-permute-start(bf16[512,128]{1,0:T(8,128)(2,1)S(1)} %get-tuple-element.146), channel_id=1, source_target_pairs={{0,96},{16,112},{32,0},{48,16},{64,32},{80,48},{96,64},{112,80},{1... | collective-permute-start | bytes 393224 | tf_op jit(solution)/shard_map/ppermute | solution.py:281
  145.0 4.4 %collective-permute-start.43 = (bf16[512,128]{1,0:T(8,128)(2,1)S(1)}, bf16[512,128]{1,0:T(8,128)(2,1)S(1)}, u32[]{:S(2)}, u32[]{:S(2)}) collective-permute-start(bf16[512,128]{1,0:T(8,128)(2,1)S(1)} %get-tuple-element.147), channel_id=1, source_target_pairs={{0,16},{16,0},{32,48},{48,32},{64,80},{80,64},{96,112},{112,96},{1... | collective-permute-start | bytes 393224 | tf_op jit(solution)/shard_map/ppermute | solution.py:270

commit v2 on v1

--- a/solution.py
+++ b/solution.py
@@ -6,7 +6,6 @@
 from jax.sharding import PartitionSpec as P
 
 TILE = 128
-BUNCH = 16
 SIDE = 2048
 BLOCK = 256
 F32 = jnp.float32
@@ -31,51 +30,29 @@
     return jnp.concatenate(values, 0)
 
 
-def dense_kernel(counts_ref, places_ref, tiles_ref, dense_ref, held_ref, arrived):
-    bunches = held_ref.shape[0] // BUNCH
-
-    def fetch(b):
-        part = pl.ds(b * BUNCH, BUNCH)
-        return pltpu.make_async_copy(tiles_ref.at[part], held_ref.at[part], arrived.at[b])
-
-    for b in range(bunches):
-        fetch(b).start()
-
+def dense_kernel(counts_ref, places_ref, tiles_ref, dense_ref):
     def clear(r, carry):
         dense_ref[pl.ds(pl.multiple_of(r * TILE, TILE), TILE), :] = jnp.zeros((TILE, SIDE), BF16)
         return carry
 
     lax.fori_loop(0, SIDE // TILE, clear, 0)
-    live = counts_ref[0]
-    for b in range(bunches):
-        fetch(b).wait()
-
-        def place(j, carry, b=b):
-            slot = b * BUNCH + j
-
-            @pl.when(slot < live)
-            def _():
-                top = pl.multiple_of(places_ref[2 * slot] * TILE, TILE)
-                left = pl.multiple_of(places_ref[2 * slot + 1] * TILE, TILE)
-                dense_ref[pl.ds(top, TILE), pl.ds(left, TILE)] = held_ref[slot]
-
-            return carry
-
-        lax.fori_loop(0, BUNCH, place, 0)
+
+    def place(slot, carry):
+        top = pl.multiple_of(places_ref[2 * slot] * TILE, TILE)
+        left = pl.multiple_of(places_ref[2 * slot + 1] * TILE, TILE)
+        dense_ref[pl.ds(top, TILE), pl.ds(left, TILE)] = tiles_ref[slot]
+        return carry
+
+    lax.fori_loop(0, counts_ref[0], place, 0)
 
 
 def dense_block(tile_values, places, tile_counts):
-    slots = tile_values.shape[0]
     smem = pl.BlockSpec(memory_space=pltpu.SMEM)
     return pl.pallas_call(
         dense_kernel,
         out_shape=jax.ShapeDtypeStruct((SIDE, SIDE), BF16),
-        in_specs=[smem, smem, pl.BlockSpec(memory_space=pltpu.HBM)],
+        in_specs=[smem, smem, WHOLE],
         out_specs=WHOLE,
-        scratch_shapes=[
-            pltpu.VMEM(tile_values.shape, BF16),
-            pltpu.SemaphoreType.DMA((slots // BUNCH,)),
-        ],
         compiler_params=pltpu.CompilerParams(vmem_limit_bytes=SCOPED),
         cost_estimate=pl.CostEstimate(flops=0, bytes_accessed=12 * MIB, transcendentals=0),
         name="dense_build",

time: 151 us -> 150 us (level)
  Pallas kernels: 19 us -> 17.3 us
    pallas_call x1, Pallas kernels: 3.54 us -> 1.85 us  [dense_block(): pl.pallas_call(dense_kernel, out_shape=jax.ShapeDtypeStruct((SIDE, SIDE),...]
    ppermute x6, waiting for transfers between devices: 2.11 us -> 3.77 us  [along_x(): return lax.ppermute(value, 'row', [(r, target(r)) for r in range(16)])]
  transfers between devices with their start and end apart: 47 -> 47, of which waited for: 21 -> 22; matrix products, arithmetic and copies ran while one was open for 1% -> 1% of each run, Pallas kernels for 11% -> 9%
where the time goes in v2:
time: 150 us
  starting transfers between devices  73.7 us (49%)
  waiting for transfers between devices  52.9 us (35%)
  Pallas kernels  17.3 us (12%)
  local copies, waits for them, and re-layouts  2.63 us (2%)
  other arithmetic  1.96 us (1%)
  between operations  1.62 us (1%)
    ppermute x18, starting transfers between devices, swap_row(): return lax.ppermute(value, 'row', [(r, r ^ mask) for r in range(16)])  36.8 us
    ppermute x16, starting transfers between devices, along_z(): return lax.ppermute(value, 'col', [(z, (z + step) % 8) for z in range(8)])  23.6 us
    ppermute x16, waiting for transfers between devices, along_z(): return lax.ppermute(value, 'col', [(z, (z + step) % 8) for z in range(8)])  17.1 us
    ppermute x18, waiting for transfers between devices, swap_row(): return lax.ppermute(value, 'row', [(r, r ^ mask) for r in range(16)])  13.5 us
    ppermute x3, waiting for transfers between devices, swap_z(): return lax.ppermute(value, 'col', [(z, z ^ mask) for z in range(8)])  11.7 us
    ppermute x6, starting transfers between devices, along_x(): return lax.ppermute(value, 'row', [(r, target(r)) for r in range(16)])  7.03 us
    pallas_call x3, Pallas kernels, rows_dot(): pl.pallas_call(lambda *refs: rows_kernel(first, stride, *refs), out_shape...  5.91 us
    ppermute x3, waiting for transfers between devices, swap_rep(): return lax.ppermute(value, 'rep', [(0, 1), (1, 0)])  5.63 us
  transfers between devices with their start and end apart: 47, of which 22 were waited for; matrix products, arithmetic and copies ran while one was open for 1% of the time, Pallas kernels for 9%

profile of v2, /device:TPU:1, one launch (start us, length us, event | category | flops | bytes accessed | tf_op | source)
XLA Modules:
  0.0 150.2 jit_solution(9079553326581551087)
XLA Ops:
  0.6 3.3 %collective-permute-start.3 = (bf16[128,512]{1,0:T(8,128)(2,1)}, bf16[128,512]{1,0:T(8,128)(2,1)S(1)}, u32[]{:S(2)}, u32[]{:S(2)}) collective-permute-start(bf16[128,512]{1,0:T(8,128)(2,1)} %refs_8_.5), channel_id=1, source_target_pairs={{0,16},{16,0},{32,48},{48,32},{64,80},{80,64},{96,112},{112,96},{1... | collective-permute-start | bytes 393224 | tf_op jit(solution)/shard_map/ppermute | solution.py:247
  4.0 0.8 collective-permute-start.2
  4.7 0.7 collective-permute-start.1
  5.4 2.2 %collective-permute-start = (bf16[128,512]{1,0:T(8,128)(2,1)}, bf16[128,512]{1,0:T(8,128)(2,1)S(1)}, u32[]{:S(2)}, u32[]{:S(2)}) collective-permute-start(bf16[128,512]{1,0:T(8,128)(2,1)} %refs_8_.5), channel_id=1, source_target_pairs={{0,128},{16,144},{32,160},{48,176},{64,192},{80,208},{96,224},{112... | collective-permute-start | bytes 393224 | tf_op jit(solution)/shard_map/ppermute | solution.py:247
  7.6 0.8 xor_add_fusion
  9.2 1.6 %collective-permute-done.1.refs_6_ = bf16[128,512]{1,0:T(8,128)(2,1)S(1)} collective-permute-done((bf16[128,512]{1,0:T(8,128)(2,1)}, bf16[128,512]{1,0:T(8,128)(2,1)S(1)}, u32[]{:S(2)}, u32[]{:S(2)}) %collective-permute-start.1) | collective-permute-done | bytes 131104 | tf_op jit(solution)/shard_map/ppermute | solution.py:258
  10.9 0.7 collective-permute-done.refs_4_
  11.6 1.6 %collective-permute-start.7 = (bf16[384,512]{1,0:T(8,128)(2,1)S(1)}, bf16[384,512]{1,0:T(8,128)(2,1)S(1)}, u32[]{:S(2)}, u32[]{:S(2)}) collective-permute-start(bf16[384,512]{1,0:T(8,128)(2,1)S(1)} %pad_maximum_fusion), channel_id=1, source_target_pairs={{0,16},{16,0},{32,48},{48,32},{64,80},{80,64},{96,112},{112,96},{1... | collective-permute-start | bytes 1179656 | tf_op jit(solution)/shard_map/ppermute | solution.py:247
  13.2 2.3 %collective-permute-start.4 = (bf16[256,512]{1,0:T(8,128)(2,1)S(1)}, bf16[256,512]{1,0:T(8,128)(2,1)S(1)}, u32[]{:S(2)}, u32[]{:S(2)}) collective-permute-start(bf16[256,512]{1,0:T(8,128)(2,1)S(1)} %pad_maximum_fusion.1), channel_id=1, source_target_pairs={{0,128},{16,144},{32,160},{48,176},{64,192},{80,208},{96,224},{112... | collective-permute-start | bytes 786440 | tf_op jit(solution)/shard_map/ppermute | solution.py:247
  15.5 1.7 %collective-permute-start.6 = (bf16[128,512]{1,0:T(8,128)(2,1)S(1)}, bf16[128,512]{1,0:T(8,128)(2,1)S(1)}, u32[]{:S(2)}, u32[]{:S(2)}) collective-permute-start(bf16[128,512]{1,0:T(8,128)(2,1)S(1)} %collective-permute-done.refs_4_), channel_id=1, source_target_pairs={{0,64},{16,80},{32,96},{48,112},{64,0},{80,16},{96,32},{112,48},{1... | collective-permute-start | bytes 393224 | tf_op jit(solution)/shard_map/ppermute | solution.py:247
  17.2 1.5 %collective-permute-start.5 = (bf16[128,512]{1,0:T(8,128)(2,1)S(1)}, bf16[128,512]{1,0:T(8,128)(2,1)S(1)}, u32[]{:S(2)}, u32[]{:S(2)}) collective-permute-start(bf16[128,512]{1,0:T(8,128)(2,1)S(1)} %collective-permute-done.1.refs_6_), channel_id=1, source_target_pairs={{0,32},{16,48},{32,64},{48,80},{64,96},{80,112},{96,0},{112,16},{1... | collective-permute-start | bytes 393224 | tf_op jit(solution)/shard_map/ppermute | solution.py:258
  19.4 2.2 %copy-done = bf16[128,128,128]{2,1,0:T(8,128)(2,1)S(1)} copy-done((bf16[128,128,128]{2,1,0:T(8,128)(2,1)S(1)}, bf16[128,128,128]{2,1,0:T(8,128)(2,1)}, u32[]{:S(2)}) %copy-start) | copy-done | bytes 4194328
  21.6 1.8 %dense_build.1.refs_0_ = bf16[2048,2048]{1,0:T(8,128)(2,1)S(1)} custom-call(s32[1]{0:T(128)S(6)} %copy.12.counts_ref, s32[256]{0:T(256)S(1)} %reshape.23.places_ref, bf16[128,128,128]{2,1,0:T(8,128)(2,1)S(1)} %copy-done), custom_call_target="tpu_custom_call" | custom-call | bytes 12582912 | tf_op jit(solution)/shard_map/dense_build/pallas_call | solution.py:51
  23.5 1.7 %collective-permute-done.5 = bf16[128,512]{1,0:T(8,128)(2,1)S(1)} collective-permute-done((bf16[128,512]{1,0:T(8,128)(2,1)S(1)}, bf16[128,512]{1,0:T(8,128)(2,1)S(1)}, u32[]{:S(2)}, u32[]{:S(2)}) %collective-permute-start.5) | collective-permute-done | bytes 131104 | tf_op jit(solution)/shard_map/ppermute | solution.py:258
  26.3 1.1 collective-permute-done.8.refs_1_
  27.4 0.7 rows_middle.1
  28.2 1.7 %collective-permute-start.9 = (bf16[128,512]{1,0:T(8,128)(2,1)S(1)}, bf16[128,512]{1,0:T(8,128)(2,1)S(1)}, u32[]{:S(2)}, u32[]{:S(2)}) collective-permute-start(bf16[128,512]{1,0:T(8,128)(2,1)S(1)} %get-tuple-element.86), channel_id=1, source_target_pairs={{0,2},{2,4},{4,6},{6,8},{8,10},{10,12},{12,14},{14,0},{1,3},{3,5},... | collective-permute-start | bytes 393224 | tf_op jit(solution)/shard_map/ppermute | solution.py:262
  29.9 4.0 %collective-permute-start.10 = (bf16[128,512]{1,0:T(8,128)(2,1)S(1)}, bf16[128,512]{1,0:T(8,128)(2,1)S(1)}, u32[]{:S(2)}, u32[]{:S(2)}) collective-permute-start(bf16[128,512]{1,0:T(8,128)(2,1)S(1)} %get-tuple-element.87), channel_id=1, source_target_pairs={{0,14},{2,0},{4,2},{6,4},{8,6},{10,8},{12,10},{14,12},{1,15},{3,1}... | collective-permute-start | bytes 393224 | tf_op jit(solution)/shard_map/ppermute | solution.py:262
  33.9 1.5 %rows_outer.1 = bf16[512,512]{1,0:T(8,128)(2,1)S(1)} custom-call(bf16[2048,2048]{1,0:T(8,128)(2,1)S(1)} %dense_build.1.refs_0_, bf16[512,512]{1,0:T(8,128)(2,1)S(1)} %collective-permute-done.8.refs_1_, bf16[512,512]{1,0:T(8,128)(2,1)S(1)} %constant_dynamic-update-slice_fusion.refs_2_, bf16[384,512]{1,0:T(8,128)(2,1)S(1)} %collective-permute-done.7.refs_3_, ...), custom_call_target="tpu_custom_call" | custom-call | flops 1073741824 | bytes 2097152 | tf_op jit(solution)/shard_map/rows_outer/pallas_call | solution.py:81
  35.5 1.9 %collective-permute-done.9 = bf16[128,512]{1,0:T(8,128)(2,1)S(1)} collective-permute-done((bf16[128,512]{1,0:T(8,128)(2,1)S(1)}, bf16[128,512]{1,0:T(8,128)(2,1)S(1)}, u32[]{:S(2)}, u32[]{:S(2)}) %collective-permute-start.9) | collective-permute-done | bytes 131104 | tf_op jit(solution)/shard_map/ppermute | solution.py:262
  37.6 2.7 %collective-permute-start.13 = (bf16[256,512]{1,0:T(8,128)(2,1)S(1)}, bf16[256,512]{1,0:T(8,128)(2,1)S(1)}, u32[]{:S(2)}, u32[]{:S(2)}) collective-permute-start(bf16[256,512]{1,0:T(8,128)(2,1)S(1)} %get-tuple-element.90), channel_id=1, source_target_pairs={{0,14},{2,0},{4,2},{6,4},{8,6},{10,8},{12,10},{14,12},{1,15},{3,1}... | collective-permute-start | bytes 786440 | tf_op jit(solution)/shard_map/ppermute | solution.py:262
  40.3 3.7 %rows_inner.1 = bf16[1280,512]{1,0:T(8,128)(2,1)S(1)} custom-call(bf16[2048,2048]{1,0:T(8,128)(2,1)S(1)} %dense_build.1.refs_0_, bf16[512,512]{1,0:T(8,128)(2,1)S(1)} %collective-permute-done.8.refs_1_, bf16[512,512]{1,0:T(8,128)(2,1)S(1)} %constant_dynamic-update-slice_fusion.refs_2_, bf16[384,512]{1,0:T(8,128)(2,1)S(1)} %collective-permute-done.7.refs_3_, ...), custom_call_target="tpu_custom_call" | custom-call | flops 2684354560 | bytes 5242880 | tf_op jit(solution)/shard_map/rows_inner/pallas_call | solution.py:81
  43.9 1.8 %collective-permute-done.12 = bf16[256,512]{1,0:T(8,128)(2,1)S(1)} collective-permute-done((bf16[256,512]{1,0:T(8,128)(2,1)S(1)}, bf16[256,512]{1,0:T(8,128)(2,1)S(1)}, u32[]{:S(2)}, u32[]{:S(2)}) %collective-permute-start.12) | collective-permute-done | bytes 262176 | tf_op jit(solution)/shard_map/ppermute | solution.py:262
  45.9 1.1 collective-permute-start.14
  47.0 1.8 %collective-permute-start.15 = (bf16[256,512]{1,0:T(8,128)(2,1)S(1)}, bf16[256,512]{1,0:T(8,128)(2,1)S(1)}, u32[]{:S(2)}, u32[]{:S(2)}) collective-permute-start(bf16[256,512]{1,0:T(8,128)(2,1)S(1)} %get-tuple-element.94), channel_id=1, source_target_pairs={{0,14},{2,0},{4,2},{6,4},{8,6},{10,8},{12,10},{14,12},{1,15},{3,1}... | collective-permute-start | bytes 786440 | tf_op jit(solution)/shard_map/ppermute | solution.py:262
  48.8 4.6 %collective-permute-done.14 = bf16[256,512]{1,0:T(8,128)(2,1)S(1)} collective-permute-done((bf16[256,512]{1,0:T(8,128)(2,1)S(1)}, bf16[256,512]{1,0:T(8,128)(2,1)S(1)}, u32[]{:S(2)}, u32[]{:S(2)}) %collective-permute-start.14) | collective-permute-done | bytes 262176 | tf_op jit(solution)/shard_map/ppermute | solution.py:262
  53.5 0.8 collective-permute-start.16
  54.3 2.0 %collective-permute-start.17 = (bf16[256,512]{1,0:T(8,128)(2,1)S(1)}, bf16[256,512]{1,0:T(8,128)(2,1)S(1)}, u32[]{:S(2)}, u32[]{:S(2)}) collective-permute-start(bf16[256,512]{1,0:T(8,128)(2,1)S(1)} %get-tuple-element.98), channel_id=1, source_target_pairs={{0,14},{2,0},{4,2},{6,4},{8,6},{10,8},{12,10},{14,12},{1,15},{3,1}... | collective-permute-start | bytes 786440 | tf_op jit(solution)/shard_map/ppermute | solution.py:262
  56.3 3.8 %collective-permute-done.16 = bf16[256,512]{1,0:T(8,128)(2,1)S(1)} collective-permute-done((bf16[256,512]{1,0:T(8,128)(2,1)S(1)}, bf16[256,512]{1,0:T(8,128)(2,1)S(1)}, u32[]{:S(2)}, u32[]{:S(2)}) %collective-permute-start.16) | collective-permute-done | bytes 262176 | tf_op jit(solution)/shard_map/ppermute | solution.py:262
  60.6 4.8 %collective-permute-done.18.theirs_ref = bf16[256,512]{1,0:T(8,128)(2,1)S(1)} collective-permute-done((bf16[256,512]{1,0:T(8,128)(2,1)S(1)}, bf16[256,512]{1,0:T(8,128)(2,1)S(1)}, u32[]{:S(2)}, u32[]{:S(2)}) %collective-permute-start.18) | collective-permute-done | bytes 262176 | tf_op jit(solution)/shard_map/ppermute | solution.py:270
  65.5 1.0 layer.1
  66.4 1.3 collective-permute-start.20
  67.7 1.4 collective-permute-start.19
  69.1 0.8 weight_part.1
  69.9 6.2 %collective-permute-start.21 = (bf16[128,512]{1,0:T(8,128)(2,1)S(1)}, bf16[128,512]{1,0:T(8,128)(2,1)S(1)}, u32[]{:S(2)}, u32[]{:S(2)}) collective-permute-start(bf16[128,512]{1,0:T(8,128)(2,1)S(1)} %get-tuple-element.108), channel_id=1, source_target_pairs={{0,16},{16,0},{32,48},{48,32},{64,80},{80,64},{96,112},{112,96},{1... | collective-permute-start | bytes 393224 | tf_op jit(solution)/shard_map/ppermute | solution.py:247
  76.1 1.0 collective-permute-done.21
  77.2 1.3 collective-permute-start.22
  79.0 1.8 %collective-permute-start.25 = (bf16[128,512]{1,0:T(8,128)(2,1)S(1)}, bf16[128,512]{1,0:T(8,128)(2,1)S(1)}, u32[]{:S(2)}, u32[]{:S(2)}) collective-permute-start(bf16[128,512]{1,0:T(8,128)(2,1)S(1)} %add_convert_fusion.12), channel_id=1, source_target_pairs={{0,64},{16,80},{32,96},{48,112},{64,0},{80,16},{96,32},{112,48},{1... | collective-permute-start | bytes 393224 | tf_op jit(solution)/shard_map/ppermute | solution.py:247
  80.7 1.2 collective-permute-start.24
  82.0 3.2 %collective-permute-done.26 = bf16[128,512]{1,0:T(8,128)(2,1)S(1)} collective-permute-done((bf16[128,512]{1,0:T(8,128)(2,1)S(1)}, bf16[128,512]{1,0:T(8,128)(2,1)S(1)}, u32[]{:S(2)}, u32[]{:S(2)}) %collective-permute-start.26) | collective-permute-done | bytes 131104 | tf_op jit(solution)/shard_map/ppermute | solution.py:247
  85.1 0.9 collective-permute-done.24
  86.1 2.5 %collective-permute-start.27 = (bf16[512,256]{1,0:T(8,128)(2,1)S(1)}, bf16[512,256]{1,0:T(8,128)(2,1)S(1)}, u32[]{:S(2)}, u32[]{:S(2)}) collective-permute-start(bf16[512,256]{1,0:T(8,128)(2,1)S(1)} %collective-permute-done.22.refs_3_), channel_id=1, source_target_pairs={{0,14},{2,0},{4,2},{6,4},{8,6},{10,8},{12,10},{14,12},{1,15},{3,1}... | collective-permute-start | bytes 786440 | tf_op jit(solution)/shard_map/ppermute | solution.py:262
  89.3 4.6 %collective-permute-done.29 = bf16[128,512]{1,0:T(8,128)(2,1)S(1)} collective-permute-done((bf16[128,512]{1,0:T(8,128)(2,1)S(1)}, bf16[128,512]{1,0:T(8,128)(2,1)S(1)}, u32[]{:S(2)}, u32[]{:S(2)}) %collective-permute-start.29) | collective-permute-done | bytes 131104 | tf_op jit(solution)/shard_map/ppermute | solution.py:247
  93.9 1.1 collective-permute-done.28.refs_7_
  95.2 2.7 %collective-permute-start.31 = (bf16[256,256]{1,0:T(8,128)(2,1)S(1)}, bf16[256,256]{1,0:T(8,128)(2,1)S(1)}, u32[]{:S(2)}, u32[]{:S(2)}) collective-permute-start(bf16[256,256]{1,0:T(8,128)(2,1)S(1)} %slice.110), channel_id=1, source_target_pairs={{0,14},{2,0},{4,2},{6,4},{8,6},{10,8},{12,10},{14,12},{1,15},{3,1}... | collective-permute-start | bytes 393224 | tf_op jit(solution)/shard_map/ppermute | solution.py:262
  97.8 4.0 %collective-permute-done.30.refs_5_ = bf16[256,256]{1,0:T(8,128)(2,1)S(1)} collective-permute-done((bf16[256,256]{1,0:T(8,128)(2,1)S(1)}, bf16[256,256]{1,0:T(8,128)(2,1)S(1)}, u32[]{:S(2)}, u32[]{:S(2)}) %collective-permute-start.30) | collective-permute-done | bytes 131104 | tf_op jit(solution)/shard_map/ppermute | solution.py:262
  102.0 1.2 columns_other.1
  103.2 10.2 %collective-permute-start.33 = (bf16[4,512,128]{2,1,0:T(8,128)(2,1)S(1)}, bf16[4,512,128]{2,1,0:T(8,128)(2,1)S(1)}, u32[]{:S(2)}, u32[]{:S(2)}) collective-permute-start(bf16[4,512,128]{2,1,0:T(8,128)(2,1)S(1)} %columns_other.1), channel_id=1, source_target_pairs={{0,16},{16,0},{32,48},{48,32},{64,80},{80,64},{96,112},{112,96},{1... | collective-permute-start | bytes 1572872 | tf_op jit(solution)/shard_map/ppermute | solution.py:247
  113.6 4.1 %columns_rest.1 = bf16[12,512,128]{2,1,0:T(8,128)(2,1)S(1)} custom-call(bf16[2048,2048]{1,0:T(8,128)(2,1)S(1)} %dense_build.1.refs_0_, bf16[512,256]{1,0:T(8,128)(2,1)S(1)} %get-tuple-element.104.refs_1_, bf16[512,256]{1,0:T(8,128)(2,1)S(1)} %collective-permute-done.19.refs_2_, bf16[512,256]{1,0:T(8,128)(2,1)S(1)} %collective-permute-done.22.refs_3_, ...), custom_call_target="tpu_custom_call" | custom-call | flops 3221225472 | bytes 6291456 | tf_op jit(solution)/shard_map/columns_rest/pallas_call | solution.py:121
  117.7 4.4 %collective-permute-done.34 = bf16[128,512]{1,0:T(8,128)(2,1)S(1)} collective-permute-done((bf16[128,512]{1,0:T(8,128)(2,1)S(1)}, bf16[128,512]{1,0:T(8,128)(2,1)S(1)}, u32[]{:S(2)}, u32[]{:S(2)}) %collective-permute-start.34) | collective-permute-done | bytes 131104 | tf_op jit(solution)/shard_map/ppermute | solution.py:266
  122.4 0.8 collective-permute-start.35
  123.2 0.7 collective-permute-start.38
  123.9 3.2 %collective-permute-start.39 = (bf16[128,512]{1,0:T(8,128)(2,1)S(1)}, bf16[128,512]{1,0:T(8,128)(2,1)S(1)}, u32[]{:S(2)}, u32[]{:S(2)}) collective-permute-start(bf16[128,512]{1,0:T(8,128)(2,1)S(1)} %add_convert_fusion.8), channel_id=1, source_target_pairs={{0,8},{2,10},{4,12},{6,14},{8,0},{10,2},{12,4},{14,6},{1,9},{3,11}... | collective-permute-start | bytes 393224 | tf_op jit(solution)/shard_map/ppermute | solution.py:266
  127.1 1.7 %collective-permute-start.37 = (bf16[512,128]{1,0:T(8,128)(2,1)S(1)}, bf16[512,128]{1,0:T(8,128)(2,1)S(1)}, u32[]{:S(2)}, u32[]{:S(2)}) collective-permute-start(bf16[512,128]{1,0:T(8,128)(2,1)S(1)} %get-tuple-element.157), channel_id=1, source_target_pairs={{0,96},{16,112},{32,0},{48,16},{64,32},{80,48},{96,64},{112,80},{1... | collective-permute-start | bytes 393224 | tf_op jit(solution)/shard_map/ppermute | solution.py:258
  128.9 7.2 %collective-permute-done.39 = bf16[128,512]{1,0:T(8,128)(2,1)S(1)} collective-permute-done((bf16[128,512]{1,0:T(8,128)(2,1)S(1)}, bf16[128,512]{1,0:T(8,128)(2,1)S(1)}, u32[]{:S(2)}, u32[]{:S(2)}) %collective-permute-start.39) | collective-permute-done | bytes 131104 | tf_op jit(solution)/shard_map/ppermute | solution.py:266
  136.3 1.0 collective-permute-start.46
  137.3 1.0 collective-permute-start.45
  138.6 2.2 %collective-permute-start.40 = (bf16[512,128]{1,0:T(8,128)(2,1)S(1)}, bf16[512,128]{1,0:T(8,128)(2,1)S(1)}, u32[]{:S(2)}, u32[]{:S(2)}) collective-permute-start(bf16[512,128]{1,0:T(8,128)(2,1)S(1)} %get-tuple-element.144), channel_id=1, source_target_pairs={{0,128},{16,144},{32,160},{48,176},{64,192},{80,208},{96,224},{112... | collective-permute-start | bytes 393224 | tf_op jit(solution)/shard_map/ppermute | solution.py:247
  141.1 1.2 collective-permute-done.46.refs_4_
  142.3 2.0 %collective-permute-start.42 = (bf16[512,128]{1,0:T(8,128)(2,1)S(1)}, bf16[512,128]{1,0:T(8,128)(2,1)S(1)}, u32[]{:S(2)}, u32[]{:S(2)}) collective-permute-start(bf16[512,128]{1,0:T(8,128)(2,1)S(1)} %get-tuple-element.146), channel_id=1, source_target_pairs={{0,96},{16,112},{32,0},{48,16},{64,32},{80,48},{96,64},{112,80},{1... | collective-permute-start | bytes 393224 | tf_op jit(solution)/shard_map/ppermute | solution.py:258
  144.3 0.8 collective-permute-done.45.refs_3_
  145.7 1.6 %weight_place.1 = f32[512,512]{1,0:T(8,128)} custom-call(s32[2]{0:T(128)S(1)} %pad_add_fusion.1.where_ref.refs_0_, bf16[128,512]{1,0:T(8,128)(2,1)S(1)} %add_convert_fusion.6.refs_1_, bf16[128,512]{1,0:T(8,128)(2,1)S(1)} %collective-permute-done.44.refs_2_, bf16[128,512]{1,0:T(8,128)(2,1)S(1)} %collective-permute-done.45.refs_3_, ...), custom_call_target="tpu_custom_call" | custom-call | tf_op jit(solution)/shard_map/weight_place/pallas_call | solution.py:236
  147.3 2.0 %collective-permute-done.40.refs_1_ = bf16[512,128]{1,0:T(8,128)(2,1)S(1)} collective-permute-done((bf16[512,128]{1,0:T(8,128)(2,1)S(1)}, bf16[512,128]{1,0:T(8,128)(2,1)S(1)}, u32[]{:S(2)}, u32[]{:S(2)}) %collective-permute-start.40) | collective-permute-done | bytes 131104 | tf_op jit(solution)/shard_map/ppermute | solution.py:247
  149.3 0.8 finish.1
  (80 shorter events, 6.8 us)
Async XLA Ops:
  0.6 8.1 %collective-permute-start.3 = (bf16[128,512]{1,0:T(8,128)(2,1)}, bf16[128,512]{1,0:T(8,128)(2,1)S(1)}, u32[]{:S(2)}, u32[]{:S(2)}) collective-permute-start(bf16[128,512]{1,0:T(8,128)(2,1)} %refs_8_.5), channel_id=1, source_target_pairs={{0,16},{16,0},{32,48},{48,32},{64,80},{80,64},{96,112},{112,96},{1... | collective-permute-start | bytes 393224 | tf_op jit(solution)/shard_map/ppermute | solution.py:247
  4.0 5.3 %collective-permute-start.2 = (bf16[128,512]{1,0:T(8,128)(2,1)}, bf16[128,512]{1,0:T(8,128)(2,1)S(1)}, u32[]{:S(2)}, u32[]{:S(2)}) collective-permute-start(bf16[128,512]{1,0:T(8,128)(2,1)} %refs_8_.5), channel_id=1, source_target_pairs={{0,96},{16,112},{32,0},{48,16},{64,32},{80,48},{96,64},{112,80},{1... | collective-permute-start | bytes 393224 | tf_op jit(solution)/shard_map/ppermute | solution.py:258
  4.7 6.1 %collective-permute-start.1 = (bf16[128,512]{1,0:T(8,128)(2,1)}, bf16[128,512]{1,0:T(8,128)(2,1)S(1)}, u32[]{:S(2)}, u32[]{:S(2)}) collective-permute-start(bf16[128,512]{1,0:T(8,128)(2,1)} %refs_8_.5), channel_id=1, source_target_pairs={{0,32},{16,48},{32,64},{48,80},{64,96},{80,112},{96,0},{112,16},{1... | collective-permute-start | bytes 393224 | tf_op jit(solution)/shard_map/ppermute | solution.py:258
  5.4 6.1 %collective-permute-start = (bf16[128,512]{1,0:T(8,128)(2,1)}, bf16[128,512]{1,0:T(8,128)(2,1)S(1)}, u32[]{:S(2)}, u32[]{:S(2)}) collective-permute-start(bf16[128,512]{1,0:T(8,128)(2,1)} %refs_8_.5), channel_id=1, source_target_pairs={{0,128},{16,144},{32,160},{48,176},{64,192},{80,208},{96,224},{112... | collective-permute-start | bytes 393224 | tf_op jit(solution)/shard_map/ppermute | solution.py:247
  11.6 13.5 %collective-permute-start.7 = (bf16[384,512]{1,0:T(8,128)(2,1)S(1)}, bf16[384,512]{1,0:T(8,128)(2,1)S(1)}, u32[]{:S(2)}, u32[]{:S(2)}) collective-permute-start(bf16[384,512]{1,0:T(8,128)(2,1)S(1)} %pad_maximum_fusion), channel_id=1, source_target_pairs={{0,16},{16,0},{32,48},{48,32},{64,80},{80,64},{96,112},{112,96},{1... | collective-permute-start | bytes 1179656 | tf_op jit(solution)/shard_map/ppermute | solution.py:247
  13.2 11.9 %collective-permute-start.4 = (bf16[256,512]{1,0:T(8,128)(2,1)S(1)}, bf16[256,512]{1,0:T(8,128)(2,1)S(1)}, u32[]{:S(2)}, u32[]{:S(2)}) collective-permute-start(bf16[256,512]{1,0:T(8,128)(2,1)S(1)} %pad_maximum_fusion.1), channel_id=1, source_target_pairs={{0,128},{16,144},{32,160},{48,176},{64,192},{80,208},{96,224},{112... | collective-permute-start | bytes 786440 | tf_op jit(solution)/shard_map/ppermute | solution.py:247
  15.5 8.0 %collective-permute-start.6 = (bf16[128,512]{1,0:T(8,128)(2,1)S(1)}, bf16[128,512]{1,0:T(8,128)(2,1)S(1)}, u32[]{:S(2)}, u32[]{:S(2)}) collective-permute-start(bf16[128,512]{1,0:T(8,128)(2,1)S(1)} %collective-permute-done.refs_4_), channel_id=1, source_target_pairs={{0,64},{16,80},{32,96},{48,112},{64,0},{80,16},{96,32},{112,48},{1... | collective-permute-start | bytes 393224 | tf_op jit(solution)/shard_map/ppermute | solution.py:247
  17.2 7.9 %collective-permute-start.5 = (bf16[128,512]{1,0:T(8,128)(2,1)S(1)}, bf16[128,512]{1,0:T(8,128)(2,1)S(1)}, u32[]{:S(2)}, u32[]{:S(2)}) collective-permute-start(bf16[128,512]{1,0:T(8,128)(2,1)S(1)} %collective-permute-done.1.refs_6_), channel_id=1, source_target_pairs={{0,32},{16,48},{32,64},{48,80},{64,96},{80,112},{96,0},{112,16},{1... | collective-permute-start | bytes 393224 | tf_op jit(solution)/shard_map/ppermute | solution.py:258
  19.4 2.2 %copy-start = (bf16[128,128,128]{2,1,0:T(8,128)(2,1)S(1)}, bf16[128,128,128]{2,1,0:T(8,128)(2,1)}, u32[]{:S(2)}) copy-start(bf16[128,128,128]{2,1,0:T(8,128)(2,1)} %tiles_ref.1) | copy-start | bytes 12582916
  21.6 4.3 %copy-start.3 = (bf16[128,512]{1,0:T(8,128)(2,1)S(1)}, bf16[128,512]{1,0:T(8,128)(2,1)}, u32[]{:S(2)}) copy-start(bf16[128,512]{1,0:T(8,128)(2,1)} %cot_ref.1) | copy-start | bytes 393220
  21.6 5.8 %copy-start.1 = (bf16[128,512]{1,0:T(8,128)(2,1)S(1)}, bf16[128,512]{1,0:T(8,128)(2,1)}, u32[]{:S(2)}) copy-start(bf16[128,512]{1,0:T(8,128)(2,1)} %refs_8_.5) | copy-start | bytes 393220
  25.2 2.2 %collective-permute-start.8 = (bf16[512,512]{1,0:T(8,128)(2,1)S(1)}, bf16[512,512]{1,0:T(8,128)(2,1)S(1)}, u32[]{:S(2)}, u32[]{:S(2)}) collective-permute-start(bf16[512,512]{1,0:T(8,128)(2,1)S(1)} %constant_dynamic-update-slice_fusion.refs_2_), channel_id=1, source_target_pairs={{0,16},{16,0},{32,48},{48,32},{64,80},{80,64},{96,112},{112,96},{1... | collective-permute-start | bytes 1572872 | tf_op jit(solution)/shard_map/ppermute | solution.py:247
  25.9 11.6 %collective-permute-start.11 = (bf16[128,512]{1,0:T(8,128)(2,1)S(1)}, bf16[128,512]{1,0:T(8,128)(2,1)S(1)}, u32[]{:S(2)}, u32[]{:S(2)}) collective-permute-start(bf16[128,512]{1,0:T(8,128)(2,1)S(1)} %copy-done.3), channel_id=1, source_target_pairs={{0,1},{1,0},{2,3},{3,2},{4,5},{5,4},{6,7},{7,6},{8,9},{9,8},{10,11... | collective-permute-start | bytes 393224 | tf_op jit(solution)/shard_map/ppermute | solution.py:270
  28.2 9.2 %collective-permute-start.9 = (bf16[128,512]{1,0:T(8,128)(2,1)S(1)}, bf16[128,512]{1,0:T(8,128)(2,1)S(1)}, u32[]{:S(2)}, u32[]{:S(2)}) collective-permute-start(bf16[128,512]{1,0:T(8,128)(2,1)S(1)} %get-tuple-element.86), channel_id=1, source_target_pairs={{0,2},{2,4},{4,6},{6,8},{8,10},{10,12},{12,14},{14,0},{1,3},{3,5},... | collective-permute-start | bytes 393224 | tf_op jit(solution)/shard_map/ppermute | solution.py:262
  29.9 7.5 %collective-permute-start.10 = (bf16[128,512]{1,0:T(8,128)(2,1)S(1)}, bf16[128,512]{1,0:T(8,128)(2,1)S(1)}, u32[]{:S(2)}, u32[]{:S(2)}) collective-permute-start(bf16[128,512]{1,0:T(8,128)(2,1)S(1)} %get-tuple-element.87), channel_id=1, source_target_pairs={{0,14},{2,0},{4,2},{6,4},{8,6},{10,8},{12,10},{14,12},{1,15},{3,1}... | collective-permute-start | bytes 393224 | tf_op jit(solution)/shard_map/ppermute | solution.py:262
  37.5 8.2 %collective-permute-start.12 = (bf16[256,512]{1,0:T(8,128)(2,1)S(1)}, bf16[256,512]{1,0:T(8,128)(2,1)S(1)}, u32[]{:S(2)}, u32[]{:S(2)}) collective-permute-start(bf16[256,512]{1,0:T(8,128)(2,1)S(1)} %get-tuple-element.89), channel_id=1, source_target_pairs={{0,2},{2,4},{4,6},{6,8},{8,10},{10,12},{12,14},{14,0},{1,3},{3,5},... | collective-permute-start | bytes 786440 | tf_op jit(solution)/shard_map/ppermute | solution.py:262
  37.6 8.1 %collective-permute-start.13 = (bf16[256,512]{1,0:T(8,128)(2,1)S(1)}, bf16[256,512]{1,0:T(8,128)(2,1)S(1)}, u32[]{:S(2)}, u32[]{:S(2)}) collective-permute-start(bf16[256,512]{1,0:T(8,128)(2,1)S(1)} %get-tuple-element.90), channel_id=1, source_target_pairs={{0,14},{2,0},{4,2},{6,4},{8,6},{10,8},{12,10},{14,12},{1,15},{3,1}... | collective-permute-start | bytes 786440 | tf_op jit(solution)/shard_map/ppermute | solution.py:262
  45.9 19.6 %copy-start.2 = (bf16[512,512]{1,0:T(8,128)(2,1)S(1)}, bf16[512,512]{1,0:T(8,128)(2,1)}, u32[]{:S(2)}) copy-start(bf16[512,512]{1,0:T(8,128)(2,1)} %weight_ref.1) | copy-start | bytes 1572868
  45.9 7.5 %collective-permute-start.14 = (bf16[256,512]{1,0:T(8,128)(2,1)S(1)}, bf16[256,512]{1,0:T(8,128)(2,1)S(1)}, u32[]{:S(2)}, u32[]{:S(2)}) collective-permute-start(bf16[256,512]{1,0:T(8,128)(2,1)S(1)} %get-tuple-element.93), channel_id=1, source_target_pairs={{0,2},{2,4},{4,6},{6,8},{8,10},{10,12},{12,14},{14,0},{1,3},{3,5},... | collective-permute-start | bytes 786440 | tf_op jit(solution)/shard_map/ppermute | solution.py:262
  47.0 6.4 %collective-permute-start.15 = (bf16[256,512]{1,0:T(8,128)(2,1)S(1)}, bf16[256,512]{1,0:T(8,128)(2,1)S(1)}, u32[]{:S(2)}, u32[]{:S(2)}) collective-permute-start(bf16[256,512]{1,0:T(8,128)(2,1)S(1)} %get-tuple-element.94), channel_id=1, source_target_pairs={{0,14},{2,0},{4,2},{6,4},{8,6},{10,8},{12,10},{14,12},{1,15},{3,1}... | collective-permute-start | bytes 786440 | tf_op jit(solution)/shard_map/ppermute | solution.py:262
  53.5 6.5 %collective-permute-start.16 = (bf16[256,512]{1,0:T(8,128)(2,1)S(1)}, bf16[256,512]{1,0:T(8,128)(2,1)S(1)}, u32[]{:S(2)}, u32[]{:S(2)}) collective-permute-start(bf16[256,512]{1,0:T(8,128)(2,1)S(1)} %get-tuple-element.97), channel_id=1, source_target_pairs={{0,2},{2,4},{4,6},{6,8},{8,10},{10,12},{12,14},{14,0},{1,3},{3,5},... | collective-permute-start | bytes 786440 | tf_op jit(solution)/shard_map/ppermute | solution.py:262
  54.3 5.7 %collective-permute-start.17 = (bf16[256,512]{1,0:T(8,128)(2,1)S(1)}, bf16[256,512]{1,0:T(8,128)(2,1)S(1)}, u32[]{:S(2)}, u32[]{:S(2)}) collective-permute-start(bf16[256,512]{1,0:T(8,128)(2,1)S(1)} %get-tuple-element.98), channel_id=1, source_target_pairs={{0,14},{2,0},{4,2},{6,4},{8,6},{10,8},{12,10},{14,12},{1,15},{3,1}... | collective-permute-start | bytes 786440 | tf_op jit(solution)/shard_map/ppermute | solution.py:262
  60.2 5.3 %collective-permute-start.18 = (bf16[256,512]{1,0:T(8,128)(2,1)S(1)}, bf16[256,512]{1,0:T(8,128)(2,1)S(1)}, u32[]{:S(2)}, u32[]{:S(2)}) collective-permute-start(bf16[256,512]{1,0:T(8,128)(2,1)S(1)} %add_convert_fusion.1.mine_ref), channel_id=1, source_target_pairs={{0,1},{1,0},{2,3},{3,2},{4,5},{5,4},{6,7},{7,6},{8,9},{9,8},{10,11... | collective-permute-start | bytes 786440 | tf_op jit(solution)/shard_map/ppermute | solution.py:270
  66.4 10.7 %collective-permute-start.20 = (bf16[512,256]{1,0:T(8,128)(2,1)S(1)}, bf16[512,256]{1,0:T(8,128)(2,1)S(1)}, u32[]{:S(2)}, u32[]{:S(2)}) collective-permute-start(bf16[512,256]{1,0:T(8,128)(2,1)S(1)} %get-tuple-element.104.refs_1_), channel_id=1, source_target_pairs={{0,2},{2,4},{4,6},{6,8},{8,10},{10,12},{12,14},{14,0},{1,3},{3,5},... | collective-permute-start | bytes 786440 | tf_op jit(solution)/shard_map/ppermute | solution.py:262
  67.7 9.4 %collective-permute-start.19 = (bf16[512,256]{1,0:T(8,128)(2,1)S(1)}, bf16[512,256]{1,0:T(8,128)(2,1)S(1)}, u32[]{:S(2)}, u32[]{:S(2)}) collective-permute-start(bf16[512,256]{1,0:T(8,128)(2,1)S(1)} %get-tuple-element.104.refs_1_), channel_id=1, source_target_pairs={{0,14},{2,0},{4,2},{6,4},{8,6},{10,8},{12,10},{14,12},{1,15},{3,1}... | collective-permute-start | bytes 786440 | tf_op jit(solution)/shard_map/ppermute | solution.py:262
  69.9 7.2 %collective-permute-start.21 = (bf16[128,512]{1,0:T(8,128)(2,1)S(1)}, bf16[128,512]{1,0:T(8,128)(2,1)S(1)}, u32[]{:S(2)}, u32[]{:S(2)}) collective-permute-start(bf16[128,512]{1,0:T(8,128)(2,1)S(1)} %get-tuple-element.108), channel_id=1, source_target_pairs={{0,16},{16,0},{32,48},{48,32},{64,80},{80,64},{96,112},{112,96},{1... | collective-permute-start | bytes 393224 | tf_op jit(solution)/shard_map/ppermute | solution.py:247
  77.2 8.9 %collective-permute-start.22 = (bf16[512,256]{1,0:T(8,128)(2,1)S(1)}, bf16[512,256]{1,0:T(8,128)(2,1)S(1)}, u32[]{:S(2)}, u32[]{:S(2)}) collective-permute-start(bf16[512,256]{1,0:T(8,128)(2,1)S(1)} %collective-permute-done.19.refs_2_), channel_id=1, source_target_pairs={{0,14},{2,0},{4,2},{6,4},{8,6},{10,8},{12,10},{14,12},{1,15},{3,1}... | collective-permute-start | bytes 786440 | tf_op jit(solution)/shard_map/ppermute | solution.py:262
  78.4 7.6 %collective-permute-start.23 = (bf16[512,256]{1,0:T(8,128)(2,1)S(1)}, bf16[512,256]{1,0:T(8,128)(2,1)S(1)}, u32[]{:S(2)}, u32[]{:S(2)}) collective-permute-start(bf16[512,256]{1,0:T(8,128)(2,1)S(1)} %collective-permute-done.20.refs_9_), channel_id=1, source_target_pairs={{0,2},{2,4},{4,6},{6,8},{8,10},{10,12},{12,14},{14,0},{1,3},{3,5},... | collective-permute-start | bytes 786440 | tf_op jit(solution)/shard_map/ppermute | solution.py:262
  78.7 6.4 %collective-permute-start.26 = (bf16[128,512]{1,0:T(8,128)(2,1)S(1)}, bf16[128,512]{1,0:T(8,128)(2,1)S(1)}, u32[]{:S(2)}, u32[]{:S(2)}) collective-permute-start(bf16[128,512]{1,0:T(8,128)(2,1)S(1)} %add_convert_fusion.12), channel_id=1, source_target_pairs={{0,96},{16,112},{32,64},{48,80},{64,32},{80,48},{96,0},{112,16},{1... | collective-permute-start | bytes 393224 | tf_op jit(solution)/shard_map/ppermute | solution.py:247
  79.0 6.2 %collective-permute-start.25 = (bf16[128,512]{1,0:T(8,128)(2,1)S(1)}, bf16[128,512]{1,0:T(8,128)(2,1)S(1)}, u32[]{:S(2)}, u32[]{:S(2)}) collective-permute-start(bf16[128,512]{1,0:T(8,128)(2,1)S(1)} %add_convert_fusion.12), channel_id=1, source_target_pairs={{0,64},{16,80},{32,96},{48,112},{64,0},{80,16},{96,32},{112,48},{1... | collective-permute-start | bytes 393224 | tf_op jit(solution)/shard_map/ppermute | solution.py:247
  80.7 5.3 %collective-permute-start.24 = (bf16[128,512]{1,0:T(8,128)(2,1)S(1)}, bf16[128,512]{1,0:T(8,128)(2,1)S(1)}, u32[]{:S(2)}, u32[]{:S(2)}) collective-permute-start(bf16[128,512]{1,0:T(8,128)(2,1)S(1)} %add_convert_fusion.12), channel_id=1, source_target_pairs={{0,32},{16,48},{32,0},{48,16},{64,96},{80,112},{96,64},{112,80},{1... | collective-permute-start | bytes 393224 | tf_op jit(solution)/shard_map/ppermute | solution.py:247
  86.1 7.8 %collective-permute-start.27 = (bf16[512,256]{1,0:T(8,128)(2,1)S(1)}, bf16[512,256]{1,0:T(8,128)(2,1)S(1)}, u32[]{:S(2)}, u32[]{:S(2)}) collective-permute-start(bf16[512,256]{1,0:T(8,128)(2,1)S(1)} %collective-permute-done.22.refs_3_), channel_id=1, source_target_pairs={{0,14},{2,0},{4,2},{6,4},{8,6},{10,8},{12,10},{14,12},{1,15},{3,1}... | collective-permute-start | bytes 786440 | tf_op jit(solution)/shard_map/ppermute | solution.py:262
  88.6 6.4 %collective-permute-start.28 = (bf16[512,256]{1,0:T(8,128)(2,1)S(1)}, bf16[512,256]{1,0:T(8,128)(2,1)S(1)}, u32[]{:S(2)}, u32[]{:S(2)}) collective-permute-start(bf16[512,256]{1,0:T(8,128)(2,1)S(1)} %collective-permute-done.23.refs_8_), channel_id=1, source_target_pairs={{0,2},{2,4},{4,6},{6,8},{8,10},{10,12},{12,14},{14,0},{1,3},{3,5},... | collective-permute-start | bytes 786440 | tf_op jit(solution)/shard_map/ppermute | solution.py:262
  88.6 5.3 %collective-permute-start.29 = (bf16[128,512]{1,0:T(8,128)(2,1)S(1)}, bf16[128,512]{1,0:T(8,128)(2,1)S(1)}, u32[]{:S(2)}, u32[]{:S(2)}) collective-permute-start(bf16[128,512]{1,0:T(8,128)(2,1)S(1)} %add_convert_fusion.11), channel_id=1, source_target_pairs={{0,128},{16,144},{32,160},{48,176},{64,192},{80,208},{96,224},{112... | collective-permute-start | bytes 393224 | tf_op jit(solution)/shard_map/ppermute | solution.py:247
  95.1 6.7 %collective-permute-start.30 = (bf16[256,256]{1,0:T(8,128)(2,1)S(1)}, bf16[256,256]{1,0:T(8,128)(2,1)S(1)}, u32[]{:S(2)}, u32[]{:S(2)}) collective-permute-start(bf16[256,256]{1,0:T(8,128)(2,1)S(1)} %slice.109), channel_id=1, source_target_pairs={{0,2},{2,4},{4,6},{6,8},{8,10},{10,12},{12,14},{14,0},{1,3},{3,5},... | collective-permute-start | bytes 393224 | tf_op jit(solution)/shard_map/ppermute | solution.py:262
  95.2 6.7 %collective-permute-start.31 = (bf16[256,256]{1,0:T(8,128)(2,1)S(1)}, bf16[256,256]{1,0:T(8,128)(2,1)S(1)}, u32[]{:S(2)}, u32[]{:S(2)}) collective-permute-start(bf16[256,256]{1,0:T(8,128)(2,1)S(1)} %slice.110), channel_id=1, source_target_pairs={{0,14},{2,0},{4,2},{6,4},{8,6},{10,8},{12,10},{14,12},{1,15},{3,1}... | collective-permute-start | bytes 393224 | tf_op jit(solution)/shard_map/ppermute | solution.py:262
  97.8 4.1 %collective-permute-start.32 = (bf16[128,512]{1,0:T(8,128)(2,1)S(1)}, bf16[128,512]{1,0:T(8,128)(2,1)S(1)}, u32[]{:S(2)}, u32[]{:S(2)}) collective-permute-start(bf16[128,512]{1,0:T(8,128)(2,1)S(1)} %add_convert_fusion.10), channel_id=1, source_target_pairs={{0,2},{2,0},{4,6},{6,4},{8,10},{10,8},{12,14},{14,12},{1,3},{3,1},... | collective-permute-start | bytes 393224 | tf_op jit(solution)/shard_map/ppermute | solution.py:266
  103.2 18.9 %collective-permute-start.33 = (bf16[4,512,128]{2,1,0:T(8,128)(2,1)S(1)}, bf16[4,512,128]{2,1,0:T(8,128)(2,1)S(1)}, u32[]{:S(2)}, u32[]{:S(2)}) collective-permute-start(bf16[4,512,128]{2,1,0:T(8,128)(2,1)S(1)} %columns_other.1), channel_id=1, source_target_pairs={{0,16},{16,0},{32,48},{48,32},{64,80},{80,64},{96,112},{112,96},{1... | collective-permute-start | bytes 1572872 | tf_op jit(solution)/shard_map/ppermute | solution.py:247
  113.4 8.7 %collective-permute-start.34 = (bf16[128,512]{1,0:T(8,128)(2,1)S(1)}, bf16[128,512]{1,0:T(8,128)(2,1)S(1)}, u32[]{:S(2)}, u32[]{:S(2)}) collective-permute-start(bf16[128,512]{1,0:T(8,128)(2,1)S(1)} %add_convert_fusion.9), channel_id=1, source_target_pairs={{0,4},{2,6},{4,0},{6,2},{8,12},{10,14},{12,8},{14,10},{1,5},{3,7},... | collective-permute-start | bytes 393224 | tf_op jit(solution)/shard_map/ppermute | solution.py:266
  122.4 13.7 %collective-permute-start.35 = (bf16[2,512,128]{2,1,0:T(8,128)(2,1)S(1)}, bf16[2,512,128]{2,1,0:T(8,128)(2,1)S(1)}, u32[]{:S(2)}, u32[]{:S(2)}) collective-permute-start(bf16[2,512,128]{2,1,0:T(8,128)(2,1)S(1)} %slice.115), channel_id=1, source_target_pairs={{0,128},{16,144},{32,160},{48,176},{64,192},{80,208},{96,224},{112... | collective-permute-start | bytes 786440 | tf_op jit(solution)/shard_map/ppermute | solution.py:247
  123.2 12.9 %collective-permute-start.38 = (bf16[3,512,128]{2,1,0:T(8,128)(2,1)S(1)}, bf16[3,512,128]{2,1,0:T(8,128)(2,1)S(1)}, u32[]{:S(2)}, u32[]{:S(2)}) collective-permute-start(bf16[3,512,128]{2,1,0:T(8,128)(2,1)S(1)} %slice.114), channel_id=1, source_target_pairs={{0,16},{16,0},{32,48},{48,32},{64,80},{80,64},{96,112},{112,96},{1... | collective-permute-start | bytes 1179656 | tf_op jit(solution)/shard_map/ppermute | solution.py:247
  123.9 12.2 %collective-permute-start.39 = (bf16[128,512]{1,0:T(8,128)(2,1)S(1)}, bf16[128,512]{1,0:T(8,128)(2,1)S(1)}, u32[]{:S(2)}, u32[]{:S(2)}) collective-permute-start(bf16[128,512]{1,0:T(8,128)(2,1)S(1)} %add_convert_fusion.8), channel_id=1, source_target_pairs={{0,8},{2,10},{4,12},{6,14},{8,0},{10,2},{12,4},{14,6},{1,9},{3,11}... | collective-permute-start | bytes 393224 | tf_op jit(solution)/shard_map/ppermute | solution.py:266
  127.1 8.9 %collective-permute-start.37 = (bf16[512,128]{1,0:T(8,128)(2,1)S(1)}, bf16[512,128]{1,0:T(8,128)(2,1)S(1)}, u32[]{:S(2)}, u32[]{:S(2)}) collective-permute-start(bf16[512,128]{1,0:T(8,128)(2,1)S(1)} %get-tuple-element.157), channel_id=1, source_target_pairs={{0,96},{16,112},{32,0},{48,16},{64,32},{80,48},{96,64},{112,80},{1... | collective-permute-start | bytes 393224 | tf_op jit(solution)/shard_map/ppermute | solution.py:258
  128.8 7.3 %collective-permute-start.36 = (bf16[512,128]{1,0:T(8,128)(2,1)S(1)}, bf16[512,128]{1,0:T(8,128)(2,1)S(1)}, u32[]{:S(2)}, u32[]{:S(2)}) collective-permute-start(bf16[512,128]{1,0:T(8,128)(2,1)S(1)} %get-tuple-element.158), channel_id=1, source_target_pairs={{0,64},{16,80},{32,96},{48,112},{64,0},{80,16},{96,32},{112,48},{1... | collective-permute-start | bytes 393224 | tf_op jit(solution)/shard_map/ppermute | solution.py:247
  136.3 5.9 %collective-permute-start.46 = (bf16[128,512]{1,0:T(8,128)(2,1)S(1)}, bf16[128,512]{1,0:T(8,128)(2,1)S(1)}, u32[]{:S(2)}, u32[]{:S(2)}) collective-permute-start(bf16[128,512]{1,0:T(8,128)(2,1)S(1)} %add_convert_fusion.6.refs_1_), channel_id=1, source_target_pairs={{0,17},{1,16},{16,1},{17,0},{32,49},{33,48},{48,33},{49,32},{64,81... | collective-permute-start | bytes 393224 | tf_op jit(solution)/shard_map/ppermute | solution.py:275
  137.3 7.7 %collective-permute-start.45 = (bf16[128,512]{1,0:T(8,128)(2,1)S(1)}, bf16[128,512]{1,0:T(8,128)(2,1)S(1)}, u32[]{:S(2)}, u32[]{:S(2)}) collective-permute-start(bf16[128,512]{1,0:T(8,128)(2,1)S(1)} %add_convert_fusion.6.refs_1_), channel_id=1, source_target_pairs={{0,1},{1,0},{2,3},{3,2},{4,5},{5,4},{6,7},{7,6},{8,9},{9,8},{10,11... | collective-permute-start | bytes 393224 | tf_op jit(solution)/shard_map/ppermute | solution.py:270
  138.3 7.4 %collective-permute-start.44 = (bf16[128,512]{1,0:T(8,128)(2,1)S(1)}, bf16[128,512]{1,0:T(8,128)(2,1)S(1)}, u32[]{:S(2)}, u32[]{:S(2)}) collective-permute-start(bf16[128,512]{1,0:T(8,128)(2,1)S(1)} %add_convert_fusion.6.refs_1_), channel_id=1, source_target_pairs={{0,16},{16,0},{32,48},{48,32},{64,80},{80,64},{96,112},{112,96},{1... | collective-permute-start | bytes 393224 | tf_op jit(solution)/shard_map/ppermute | solution.py:247
  138.6 10.8 %collective-permute-start.40 = (bf16[512,128]{1,0:T(8,128)(2,1)S(1)}, bf16[512,128]{1,0:T(8,128)(2,1)S(1)}, u32[]{:S(2)}, u32[]{:S(2)}) collective-permute-start(bf16[512,128]{1,0:T(8,128)(2,1)S(1)} %get-tuple-element.144), channel_id=1, source_target_pairs={{0,128},{16,144},{32,160},{48,176},{64,192},{80,208},{96,224},{112... | collective-permute-start | bytes 393224 | tf_op jit(solution)/shard_map/ppermute | solution.py:247
  140.7 8.6 %collective-permute-start.41 = (bf16[512,128]{1,0:T(8,128)(2,1)S(1)}, bf16[512,128]{1,0:T(8,128)(2,1)S(1)}, u32[]{:S(2)}, u32[]{:S(2)}) collective-permute-start(bf16[512,128]{1,0:T(8,128)(2,1)S(1)} %fusion.2), channel_id=1, source_target_pairs={{0,32},{16,48},{32,64},{48,80},{64,96},{80,112},{96,0},{112,16},{1... | collective-permute-start | bytes 393224 | tf_op jit(solution)/shard_map/ppermute | solution.py:258
  142.3 7.1 %collective-permute-start.42 = (bf16[512,128]{1,0:T(8,128)(2,1)S(1)}, bf16[512,128]{1,0:T(8,128)(2,1)S(1)}, u32[]{:S(2)}, u32[]{:S(2)}) collective-permute-start(bf16[512,128]{1,0:T(8,128)(2,1)S(1)} %get-tuple-element.146), channel_id=1, source_target_pairs={{0,96},{16,112},{32,0},{48,16},{64,32},{80,48},{96,64},{112,80},{1... | collective-permute-start | bytes 393224 | tf_op jit(solution)/shard_map/ppermute | solution.py:258
  145.1 4.3 %collective-permute-start.43 = (bf16[512,128]{1,0:T(8,128)(2,1)S(1)}, bf16[512,128]{1,0:T(8,128)(2,1)S(1)}, u32[]{:S(2)}, u32[]{:S(2)}) collective-permute-start(bf16[512,128]{1,0:T(8,128)(2,1)S(1)} %get-tuple-element.147), channel_id=1, source_target_pairs={{0,16},{16,0},{32,48},{48,32},{64,80},{80,64},{96,112},{112,96},{1... | collective-permute-start | bytes 393224 | tf_op jit(solution)/shard_map/ppermute | solution.py:247
